TPU v7x, 512 devices: a whole 4x8x8 slice. The times are simulated.
512 devices in a mesh: ctx: 64 (over x, y, core), head: 8 (over z).
Axes of the slice: x: 4, y: 8, z: 8, core: 2. Of those that a mesh axis runs over, the one named last changes fastest.
Arguments:
- queries: bfloat16 [32768, 4096], P(('ctx', 'head')), may hold values from -48 to 48
- keys: bfloat16 [32768, 4096], P(('ctx', 'head')), may hold values from -6 to 6
- values: bfloat16 [32768, 4096], P(('ctx', 'head')), may hold values from -6 to 6
- rates: float32 [32768, 8], P('ctx', 'head'), may hold values from 0.00016572815 to 0.0016572815
- fast_gate: float32 [8, 512, 512], P('head'), may hold values from -0.25 to 0.25
- fast_up: float32 [8, 512, 512], P('head'), may hold values from -0.25 to 0.25
- fast_down: float32 [8, 512, 512], P('head'), may hold values from -0.25 to 0.25
- out_gain: float32 [4096], P('head'), may hold values from 0.5 to 1.5
Outputs:
- mixed: bfloat16 [32768, 4096], P('ctx', 'head')
All inputs are finite; a program needn't handle non-finite values.
Results may differ from a plain program's by a relative error of at most 0.012.
Values may be sent and summed in bfloat16 or wider, within the bound.
A program may use at most 64 MiB of HBM per device.

v0:
```python
import math

import jax
import jax.numpy as jnp
from jax import lax
from jax.sharding import Mesh
from jax.sharding import PartitionSpec as P

WINDOW = 1024
AHD = 128
FD = 512
CTX = ("ctx_0", "ctx_1", "ctx_2")
CTX_HEAD = ("ctx_0", "ctx_1", "ctx_2", "head")


epsilon = 1e-06
rms_epsilon = 1e-05


def passed_along(value, axis, steps):
    count = lax.axis_size(axis)
    first, last = (max(0, -steps), min(count, count - steps))
    return lax.ppermute(value, axis, [(source, source + steps) for source in range(first, last)])


def in_blocks(value, dim, peers):
    lengths = value.shape
    parts = value.reshape(*lengths[:dim], peers, lengths[dim] // peers, *lengths[dim + 1 :])
    return jnp.moveaxis(parts, dim, 0)


def summed_on_arrival(value, axis, dim):
    peers = lax.axis_size(axis)
    parts = lax.all_to_all(in_blocks(value, dim, peers), axis, 0, 0, tiled=True)
    return jnp.sum(parts, axis=0)


def sum_by_axis(value, axes, dim):
    far, near = axes
    own = summed_on_arrival(in_blocks(value, dim, lax.axis_size(far)), near, dim + 1)
    return jnp.sum(lax.all_to_all(own, far, 0, 0, tiled=True), axis=0)


def sent_together(arrays, axis, dim, along):
    ends, at = ([], 0)
    for a in arrays[:-1]:
        at += a.shape[along]
        ends.append(at)
    both = jnp.concatenate(arrays, axis=along)
    return tuple(jnp.split(sum_by_axis(both, axis, dim), ends, axis=along))


def over_axes(value, axes):
    for axis in axes:
        value = lax.psum(value, axis)
    return value


def copy_for_each(value, axis):
    peers = lax.axis_size(axis)
    return lax.all_to_all(
        jnp.broadcast_to(value[None], (peers, *value.shape)), axis, 0, 0, tiled=True
    )


def in_order(parts, dim):
    parts = jnp.moveaxis(parts, 0, dim)
    lengths = parts.shape
    return parts.reshape(*lengths[:dim], lengths[dim] * lengths[dim + 1], *lengths[dim + 2 :])


def gathered_by_axis(value, axes, dim):
    far, near = axes
    parts = copy_for_each(copy_for_each(value, far), near)
    return in_order(parts.swapaxes(0, 1).reshape(-1, *value.shape), dim)


def in_one_piece(arrays, axis, dim, along):
    widths = [a.shape[along] for a in arrays]
    both = jnp.concatenate(arrays, axis=along)
    filled = gathered_by_axis(both, axis, dim)
    return tuple(jnp.split(filled, [sum(widths[:k]) for k in range(1, len(widths))], axis=along))


def silu_slope(pre):
    sigma = jax.nn.sigmoid(pre)
    return sigma * (1.0 + pre * (1.0 - sigma))


def column_norms(matrix):
    return jnp.sqrt(jnp.sum(matrix * matrix, axis=-2) + epsilon)


def shards(queries, keys, values, rates, fast_gate, fast_up, fast_down, out_gain):
    query_here, key_here, value_here = (
        lax.all_to_all(queries, "head", split_axis=1, concat_axis=0, tiled=True),
        lax.all_to_all(keys, "head", split_axis=1, concat_axis=0, tiled=True),
        lax.all_to_all(values, "head", split_axis=1, concat_axis=0, tiled=True),
    )
    token_count = query_here.shape[0]
    width_here = query_here.shape[1]
    reach = WINDOW // token_count
    first_token = lax.axis_index(CTX) * token_count
    paired = jnp.stack([key_here, value_here])
    earlier = []
    for distance in range(reach, 0, -1):
        earlier.append(passed_along(paired, CTX, distance))
    collected = jnp.concatenate(earlier + [paired], axis=1)
    heads_here = width_here // AHD
    span_keys = (reach + 1) * token_count
    query_heads = query_here.reshape(token_count, heads_here, AHD)
    key_heads = collected[0].reshape(span_keys, heads_here, AHD)
    value_heads = collected[1].reshape(span_keys, heads_here, AHD)
    scores = jnp.einsum(
        "qhd,khd->hqk", query_heads, key_heads, preferred_element_type=jnp.float32
    ) * (1.0 / math.sqrt(AHD))
    query_pos = first_token + jnp.arange(token_count, dtype=jnp.int32)
    key_pos = first_token - reach * token_count + jnp.arange(span_keys, dtype=jnp.int32)
    allowed = (
        (key_pos[None, :] <= query_pos[:, None])
        & (key_pos[None, :] > query_pos[:, None] - WINDOW)
        & (key_pos[None, :] >= 0)
    )
    scores = jnp.where(allowed[None], scores, -1e30)
    peak = jnp.max(scores, axis=-1, keepdims=True)
    expo = jnp.exp(scores - peak)
    weights = (expo / jnp.sum(expo, axis=-1, keepdims=True)).astype(jnp.bfloat16)
    attended = jnp.einsum(
        "hqk,khd->qhd", weights, value_heads, preferred_element_type=jnp.float32
    ).reshape(token_count, width_here)
    fast_here = width_here // FD
    query_fast = query_here.reshape(token_count, fast_here, FD)
    key_fast = key_here.reshape(token_count, fast_here, FD)
    value_fast = value_here.reshape(token_count, fast_here, FD)
    gate_cast = fast_gate.astype(jnp.bfloat16)
    up_cast = fast_up.astype(jnp.bfloat16)
    down_cast = fast_down.astype(jnp.bfloat16)
    pre_gate = jnp.einsum("thi,hij->thj", key_fast, gate_cast, preferred_element_type=jnp.float32)
    pre_up = jnp.einsum("thi,hij->thj", key_fast, up_cast, preferred_element_type=jnp.float32)
    hidden = (jax.nn.silu(pre_gate) * pre_up).astype(jnp.bfloat16)
    target = (rates[:, :, None] * value_fast.astype(jnp.float32)).astype(jnp.bfloat16)
    step_down = jnp.einsum("thi,thj->hij", hidden, target, preferred_element_type=jnp.float32)
    back = jnp.einsum("thj,hij->thi", target, down_cast, preferred_element_type=jnp.float32)
    grad_gate = (back * pre_up * silu_slope(pre_gate)).astype(jnp.bfloat16)
    grad_up = (back * jax.nn.silu(pre_gate)).astype(jnp.bfloat16)
    step_gate = jnp.einsum("thi,thj->hij", key_fast, grad_gate, preferred_element_type=jnp.float32)
    step_up = jnp.einsum("thi,thj->hij", key_fast, grad_up, preferred_element_type=jnp.float32)
    initials = (fast_gate, fast_up, fast_down)
    initial_norms = [column_norms(matrix) for matrix in initials]
    shares = sent_together((step_gate, step_up, step_down), (("ctx_0", "ctx_1"), "ctx_2"), 1, 0)
    row_count = shares[0].shape[1]
    row_start = lax.axis_index(CTX) * row_count
    moved_rows = [
        lax.dynamic_slice_in_dim(initial, row_start, row_count, 1) + share
        for initial, share in zip(initials, shares)
    ]
    squares = jax.tree.map(
        lambda part: over_axes(part, CTX),
        tuple((jnp.sum(rows_part * rows_part, axis=1) for rows_part in moved_rows)),
    )
    pieces = []
    for rows_part, norm_before, square_sum in zip(moved_rows, initial_norms, squares):
        pieces.append(
            (rows_part * (norm_before / jnp.sqrt(square_sum + epsilon))[:, None, :]).astype(
                jnp.bfloat16
            )
        )
    renormed = in_one_piece((pieces[0], pieces[1], pieces[2]), (("ctx_0", "ctx_1"), "ctx_2"), 1, 0)
    read_gate = jnp.einsum(
        "thi,hij->thj", query_fast, renormed[0], preferred_element_type=jnp.float32
    )
    read_up = jnp.einsum(
        "thi,hij->thj", query_fast, renormed[1], preferred_element_type=jnp.float32
    )
    read_hidden = (jax.nn.silu(read_gate) * read_up).astype(jnp.bfloat16)
    read = jnp.einsum("thi,hij->thj", read_hidden, renormed[2], preferred_element_type=jnp.float32)
    scale_back = lax.rsqrt(jnp.mean(read * read, axis=-1, keepdims=True) + rms_epsilon)
    readout = read * scale_back * out_gain.reshape(fast_here, FD)[None, :, :]
    return (attended + readout.reshape(token_count, width_here)).astype(jnp.bfloat16)


def solution(mesh):
    finer = Mesh(
        mesh.devices.reshape(4, 8, 2, mesh.shape["head"]), ("ctx_0", "ctx_1", "ctx_2", "head")
    )
    return jax.shard_map(
        shards,
        mesh=finer,
        in_specs=(
            P(CTX_HEAD, None),
            P(CTX_HEAD, None),
            P(CTX_HEAD, None),
            P(CTX, "head"),
            P("head", None, None),
            P("head", None, None),
            P("head", None, None),
            P("head"),
        ),
        out_specs=P(CTX, "head"),
        check_vma=False,
    )
```

profile of v0, /device:TPU:1, one launch (start us, length us, event | category | flops | bytes accessed | tf_op | source)
XLA Modules:
  0.0 256.8 jit_solution(16047262668846797929)
XLA Ops:
  0.0 2.0 copy.126
  2.0 10.9 %all-to-all-start = ((bf16[64,8,512]{2,0,1:T(8,128)(2,1)}), bf16[64,8,512]{2,0,1:T(8,128)(2,1)S(1)}, u32[]{:S(2)}, u32[]{:S(2)}) async-start(bf16[64,8,512]{2,0,1:T(8,128)(2,1)} %bitcast.169), calls=%async_computation | async-start | bytes 1048576 | tf_op jit(solution)/shard_map/all_to_all | solution.py:97
  12.9 1.9 copy.125
  14.8 16.1 %all-to-all-done = bf16[64,8,512]{2,0,1:T(8,128)(2,1)S(1)} async-done(((bf16[64,8,512]{2,0,1:T(8,128)(2,1)}), bf16[64,8,512]{2,0,1:T(8,128)(2,1)S(1)}, u32[]{:S(2)}, u32[]{:S(2)}) %all-to-all-start) | async-done | bytes 524320 | tf_op jit(solution)/shard_map/all_to_all | solution.py:97
  30.8 3.5 %all-to-all-start.1 = ((bf16[64,8,512]{2,0,1:T(8,128)(2,1)}), bf16[64,8,512]{2,0,1:T(8,128)(2,1)S(1)}, u32[]{:S(2)}, u32[]{:S(2)}) async-start(bf16[64,8,512]{2,0,1:T(8,128)(2,1)} %bitcast.168), calls=%async_computation.1 | async-start | bytes 1048576 | tf_op jit(solution)/shard_map/all_to_all | solution.py:98
  34.3 0.0 copy-done.5
  34.3 0.8 copy.124
  35.2 0.0 copy-done
  35.2 0.4 convolution_bitcast_fusion.2
  35.6 0.0 copy-start.1
  35.6 0.0 copy-start.6
  35.6 2.0 convolution_bitcast_fusion.3
  37.7 0.0 copy-done.1
  37.7 0.0 copy-start.3
  37.7 1.0 copy-done.3
  38.7 0.3 fusion.17
  39.0 13.2 %all-to-all-done.1 = bf16[64,8,512]{2,0,1:T(8,128)(2,1)S(1)} async-done(((bf16[64,8,512]{2,0,1:T(8,128)(2,1)}), bf16[64,8,512]{2,0,1:T(8,128)(2,1)S(1)}, u32[]{:S(2)}, u32[]{:S(2)}) %all-to-all-start.1) | async-done | bytes 524320 | tf_op jit(solution)/shard_map/all_to_all | solution.py:98
  52.2 0.0 copy-done.6
  52.2 1.7 convolution_bitcast_fusion.6
  53.9 3.4 %fusion.19 = f32[512,512]{0,1:T(8,128)} fusion(bf16[512,512]{1,0:T(8,128)(2,1)S(1)} %bitcast.172, f32[512,1,512]{2,0,1:T(8,128)} %copy-done.1, f32[512,1,512]{2,0,1:T(8,128)S(1)} %convolution_bitcast_fusion.6, f32[512,1,512]{2,0,1:T(8,128)} %copy-done.3), kind=kOutput, calls=%fused_computation.48 | convolution fusion | flops 271056896 | bytes 4718592 | tf_op jit(solution)/shard_map/thi,thj->hij/dot_general | solution.py:146
  57.3 1.6 fusion.15
  58.9 0.2 copy.90
  59.1 0.5 convolution_bitcast_fusion.5
  59.7 1.9 copy_bitcast_fusion
  61.6 7.3 %all_to_all.68 = f32[2,32,3,8,512]{4,3,1,2,0:T(8,128)} all-to-all(f32[2,32,3,8,512]{4,3,1,2,0:T(8,128)S(1)} %copy_bitcast_fusion), channel_id=1, replica_groups=mesh['ctx_0'=4,'ctx_1'=8,'ctx_2'=2,'head'=8] {'ctx_2'}, dimensions={0} | all-to-all | bytes 6291456 | tf_op jit(solution)/shard_map/all_to_all | solution.py:34
  68.9 3.5 %all-to-all-start.2 = ((bf16[64,8,512]{2,0,1:T(8,128)(2,1)}), bf16[64,8,512]{2,0,1:T(8,128)(2,1)S(1)}, u32[]{:S(2)}, u32[]{:S(2)}) async-start(bf16[64,8,512]{2,0,1:T(8,128)(2,1)} %bitcast.167), calls=%async_computation.2 | async-start | bytes 1048576 | tf_op jit(solution)/shard_map/all_to_all | solution.py:96
  72.4 0.1 multiply_reduce_fusion.3
  72.5 1.3 multiply_reduce_fusion.2
  73.9 1.3 multiply_reduce_fusion.1
  75.2 2.4 reduce_sum.97
  77.6 1.3 copy.93
  78.9 11.4 %all-to-all-done.2 = bf16[64,8,512]{2,0,1:T(8,128)(2,1)S(1)} async-done(((bf16[64,8,512]{2,0,1:T(8,128)(2,1)}), bf16[64,8,512]{2,0,1:T(8,128)(2,1)S(1)}, u32[]{:S(2)}, u32[]{:S(2)}) %all-to-all-start.2) | async-done | bytes 524320 | tf_op jit(solution)/shard_map/all_to_all | solution.py:96
  90.3 9.7 %all-to-all-start.4 = ((f32[32,3,8,512]{3,2,1,0:T(8,128)}), f32[32,3,8,512]{3,2,1,0:T(8,128)S(1)}, u32[]{:S(2)}, u32[]{:S(2)}) async-start(f32[32,3,8,512]{3,2,1,0:T(8,128)} %copy.93), calls=%async_computation.4 | async-start | bytes 3145728 | tf_op jit(solution)/shard_map/all_to_all | solution.py:41
  100.0 1.1 pad_maximum_fusion
  101.1 4.0 %collective-permute-start.1 = (bf16[2,512,512]{2,1,0:T(8,128)(2,1)}, bf16[2,512,512]{2,1,0:T(8,128)(2,1)}, u32[]{:S(2)}, u32[]{:S(2)}) collective-permute-start(bf16[2,512,512]{2,1,0:T(8,128)(2,1)} %pad_maximum_fusion), channel_id=1, source_target_pairs={{0,8},{8,16},{16,24},{24,32},{32,40},{40,48},{48,56},{56,64},{64,7... | collective-permute-start | bytes 3145736 | tf_op jit(solution)/shard_map/ppermute | solution.py:23
  105.2 4.1 %collective-permute-start = (bf16[2,512,512]{2,1,0:T(8,128)(2,1)}, bf16[2,512,512]{2,1,0:T(8,128)(2,1)}, u32[]{:S(2)}, u32[]{:S(2)}) collective-permute-start(bf16[2,512,512]{2,1,0:T(8,128)(2,1)} %pad_maximum_fusion), channel_id=1, source_target_pairs={{0,16},{8,24},{16,32},{24,40},{32,48},{40,56},{48,64},{56,72},{64,... | collective-permute-start | bytes 3145736 | tf_op jit(solution)/shard_map/ppermute | solution.py:23
  109.3 1.9 and_and_fusion
  111.2 0.9 reshape.348
  112.1 43.8 %collective-permute-done.1 = bf16[2,512,512]{2,1,0:T(8,128)(2,1)} collective-permute-done((bf16[2,512,512]{2,1,0:T(8,128)(2,1)}, bf16[2,512,512]{2,1,0:T(8,128)(2,1)}, u32[]{:S(2)}, u32[]{:S(2)}) %collective-permute-start.1) | collective-permute-done | bytes 1048608 | tf_op jit(solution)/shard_map/ppermute | solution.py:23
  155.9 12.2 %collective-permute-done = bf16[2,512,512]{2,1,0:T(8,128)(2,1)} collective-permute-done((bf16[2,512,512]{2,1,0:T(8,128)(2,1)}, bf16[2,512,512]{2,1,0:T(8,128)(2,1)}, u32[]{:S(2)}, u32[]{:S(2)}) %collective-permute-start) | collective-permute-done | bytes 1048608 | tf_op jit(solution)/shard_map/ppermute | solution.py:23
  168.0 1.7 maximum_maximum_fusion
  169.7 1.9 fusion.44
  171.6 2.7 %copy.83 = bf16[1,1536,512]{1,2,0:T(8,128)(2,1)} copy(bf16[1,1536,512]{2,1,0:T(8,128)(2,1)} %get-tuple-element.17) | data formatting | bytes 3145728 | tf_op jit(solution)/shard_map/slice | solution.py:112
  174.2 2.6 %copy.82 = bf16[1,1536,512]{1,2,0:T(8,128)(2,1)} copy(bf16[1,1536,512]{2,1,0:T(8,128)(2,1)} %get-tuple-element.18) | data formatting | bytes 3145728 | tf_op jit(solution)/shard_map/slice | solution.py:113
  176.8 0.0 copy-done.4
  176.8 10.9 %fusion.45 = (f32[4,512]{1,0:T(4,128)S(1)}, f32[4,512,1536]{1,2,0:T(8,128)}) fusion(pred[512,1536]{0,1:T(8,128)(4,1)S(1)} %copy-done.4, bf16[1536,4,128]{0,2,1:T(8,128)(2,1)} %bitcast.187, bf16[512,4,128]{2,1,0:T(4,128)(2,1)} %reshape.348), kind=kOutput, calls=%fused_computation.88 | convolution fusion | flops 817890816 | bytes 15474688 | tf_op jit(solution)/shard_map/sub | solution.py:126
  187.7 0.0 all-to-all-done.4
  187.7 0.1 reduce_sum.98
  187.8 0.8 multiply_reduce_fusion.6
  188.6 11.8 %all-reduce.1 = (f32[1,512]{1,0:T(1,128)S(1)}, f32[1,512]{1,0:T(1,128)S(1)}, f32[1,512]{1,0:T(1,128)S(1)}) all-reduce(f32[1,512]{1,0:T(1,128)S(1)} %bitcast.197, f32[1,512]{1,0:T(1,128)S(1)} %bitcast.198, f32[1,512]{1,0:T(1,128)S(1)} %bitcast.196), channel_id=1, replica_groups=mesh['ctx_0'=4,'ctx_1'=8,'ctx_2'=2,'head'=8] {'ctx_0'}, use_global_device_ids=true, to_apply=%region_16.17 | all-reduce | flops 1536 | bytes 12288 | tf_op jit(solution)/shard_map/psum | solution.py:55
  200.4 11.9 %all-reduce = (f32[1,512]{1,0:T(1,128)S(1)}, f32[1,512]{1,0:T(1,128)S(1)}, f32[1,512]{1,0:T(1,128)S(1)}) all-reduce(f32[1,512]{1,0:T(1,128)S(1)} %get-tuple-element.11, f32[1,512]{1,0:T(1,128)S(1)} %get-tuple-element.12, f32[1,512]{1,0:T(1,128)S(1)} %get-tuple-element.13), channel_id=1, replica_groups=mesh['ctx_0'=4,'ctx_1'=8,'ctx_2'=2,'head'=8] {'ctx_1'}, use_global_device_ids=true, to_apply=%region_17.18 | all-reduce | flops 1536 | bytes 12288 | tf_op jit(solution)/shard_map/psum | solution.py:55
  212.3 2.5 all-reduce.2
  214.8 0.8 multiply_convert_fusion.6
  215.6 1.0 broadcast_in_dim.18
  216.6 4.9 %all-to-all-start.5 = ((bf16[32,3,8,512]{3,2,1,0:T(8,128)(2,1)}), bf16[32,3,8,512]{3,2,1,0:T(8,128)(2,1)S(1)}, u32[]{:S(2)}, u32[]{:S(2)}) async-start(bf16[32,3,8,512]{3,2,1,0:T(8,128)(2,1)} %broadcast_in_dim.18), calls=%async_computation.5 | async-start | bytes 1572864 | tf_op jit(solution)/shard_map/all_to_all | solution.py:61
  221.5 6.1 %fusion.5 = f32[4,128,512]{2,1,0:T(8,128)S(1)} fusion(bf16[1536,4,128]{0,2,1:T(8,128)(2,1)} %bitcast.186, f32[4,512,1536]{1,2,0:T(8,128)} %get-tuple-element.23, f32[4,512]{1,0:T(4,128)S(1)} %get-tuple-element.22), kind=kOutput, calls=%fused_computation.8 | convolution fusion | flops 811597824 | bytes 15212544 | tf_op jit(solution)/shard_map/hqk,khd->qhd/dot_general | solution.py:128
  227.6 13.6 %all-to-all-done.5 = bf16[32,3,8,512]{3,2,1,0:T(8,128)(2,1)S(1)} async-done(((bf16[32,3,8,512]{3,2,1,0:T(8,128)(2,1)}), bf16[32,3,8,512]{3,2,1,0:T(8,128)(2,1)S(1)}, u32[]{:S(2)}, u32[]{:S(2)}) %all-to-all-start.5) | async-done | bytes 786464 | tf_op jit(solution)/shard_map/all_to_all | solution.py:61
  241.2 0.1 broadcast_in_dim.19
  241.3 8.2 %all_to_all.69 = bf16[2,32,3,8,512]{4,3,2,1,0:T(8,128)(2,1)S(1)} all-to-all(bf16[2,32,3,8,512]{4,3,2,1,0:T(8,128)(2,1)S(1)} %broadcast_in_dim.19), channel_id=1, replica_groups=mesh['ctx_0'=4,'ctx_1'=8,'ctx_2'=2,'head'=8] {'ctx_2'}, dimensions={0} | all-to-all | bytes 3145728 | tf_op jit(solution)/shard_map/all_to_all | solution.py:61
  249.5 0.2 copy.94
  249.7 1.4 convolution_bitcast_fusion.1
  251.1 3.2 %multiply_reduce_fusion = (f32[512]{0:T(512)S(1)}, f32[1,512,512]{2,1,0:T(8,128)}) fusion(bf16[512,512]{1,0:T(8,128)(2,1)S(1)} %bitcast.182, f32[512,1,512]{2,0,1:T(8,128)} %convolution_bitcast_fusion.1, bf16[3,64,8,512]{3,2,0,1:T(8,128)(2,1)S(1)} %bitcast.184), kind=kOutput, calls=%fused_computation.29 | convolution fusion | flops 538967552 | bytes 3672064 | tf_op jit(solution)/shard_map/thi,hij->thj/dot_general | solution.py:176
  254.3 1.5 fusion.11
  255.8 1.0 copy.97
  (17 shorter events, 0.1 us)
Async XLA Ops:
  0.0 34.3 %copy-start.5 = (bf16[64,4096]{1,0:T(8,128)(2,1)S(1)}, bf16[64,4096]{1,0:T(8,128)(2,1)}, u32[]{:S(2)}) copy-start(bf16[64,4096]{1,0:T(8,128)(2,1)} %param.8) | copy-start | bytes 1572868
  0.0 35.2 %copy-start = (f32[1,512,512]{2,1,0:T(8,128)S(1)}, f32[1,512,512]{2,1,0:T(8,128)}, u32[]{:S(2)}) copy-start(f32[1,512,512]{2,1,0:T(8,128)} %param.12) | copy-start | bytes 3145732
  2.0 28.8 %all-to-all-start = ((bf16[64,8,512]{2,0,1:T(8,128)(2,1)}), bf16[64,8,512]{2,0,1:T(8,128)(2,1)S(1)}, u32[]{:S(2)}, u32[]{:S(2)}) async-start(bf16[64,8,512]{2,0,1:T(8,128)(2,1)} %bitcast.169), calls=%async_computation | async-start | bytes 1048576 | tf_op jit(solution)/shard_map/all_to_all | solution.py:97
  30.8 21.4 %all-to-all-start.1 = ((bf16[64,8,512]{2,0,1:T(8,128)(2,1)}), bf16[64,8,512]{2,0,1:T(8,128)(2,1)S(1)}, u32[]{:S(2)}, u32[]{:S(2)}) async-start(bf16[64,8,512]{2,0,1:T(8,128)(2,1)} %bitcast.168), calls=%async_computation.1 | async-start | bytes 1048576 | tf_op jit(solution)/shard_map/all_to_all | solution.py:98
  35.6 2.1 copy-start.1
  35.6 16.6 %copy-start.6 = (f32[512,1]{0,1:T(1,128)S(1)}, f32[512,1]{0,1:T(1,128)}, u32[]{:S(2)}) copy-start(f32[512,1]{0,1:T(1,128)} %param.11) | copy-start | bytes 6148
  37.7 1.0 copy-start.3
  53.9 3.4 %copy-start.2 = (f32[512,1,512]{2,0,1:T(8,128)S(1)}, f32[512,1,512]{2,0,1:T(8,128)}, u32[]{:S(2)}) copy-start(f32[512,1,512]{2,0,1:T(8,128)} %copy-done.1) | copy-start | bytes 3145732
  68.9 21.4 %all-to-all-start.2 = ((bf16[64,8,512]{2,0,1:T(8,128)(2,1)}), bf16[64,8,512]{2,0,1:T(8,128)(2,1)S(1)}, u32[]{:S(2)}, u32[]{:S(2)}) async-start(bf16[64,8,512]{2,0,1:T(8,128)(2,1)} %bitcast.167), calls=%async_computation.2 | async-start | bytes 1048576 | tf_op jit(solution)/shard_map/all_to_all | solution.py:96
  90.3 97.4 %all-to-all-start.4 = ((f32[32,3,8,512]{3,2,1,0:T(8,128)}), f32[32,3,8,512]{3,2,1,0:T(8,128)S(1)}, u32[]{:S(2)}, u32[]{:S(2)}) async-start(f32[32,3,8,512]{3,2,1,0:T(8,128)} %copy.93), calls=%async_computation.4 | async-start | bytes 3145728 | tf_op jit(solution)/shard_map/all_to_all | solution.py:41
  101.1 54.7 %collective-permute-start.1 = (bf16[2,512,512]{2,1,0:T(8,128)(2,1)}, bf16[2,512,512]{2,1,0:T(8,128)(2,1)}, u32[]{:S(2)}, u32[]{:S(2)}) collective-permute-start(bf16[2,512,512]{2,1,0:T(8,128)(2,1)} %pad_maximum_fusion), channel_id=1, source_target_pairs={{0,8},{8,16},{16,24},{24,32},{32,40},{40,48},{48,56},{56,64},{64,7... | collective-permute-start | bytes 3145736 | tf_op jit(solution)/shard_map/ppermute | solution.py:23
  105.2 62.8 %collective-permute-start = (bf16[2,512,512]{2,1,0:T(8,128)(2,1)}, bf16[2,512,512]{2,1,0:T(8,128)(2,1)}, u32[]{:S(2)}, u32[]{:S(2)}) collective-permute-start(bf16[2,512,512]{2,1,0:T(8,128)(2,1)} %pad_maximum_fusion), channel_id=1, source_target_pairs={{0,16},{8,24},{16,32},{24,40},{32,48},{40,56},{48,64},{56,72},{64,... | collective-permute-start | bytes 3145736 | tf_op jit(solution)/shard_map/ppermute | solution.py:23
  171.6 5.3 %copy-start.4 = (pred[512,1536]{0,1:T(8,128)(4,1)S(1)}, pred[512,1536]{0,1:T(8,128)(4,1)}, u32[]{:S(2)}) copy-start(pred[512,1536]{0,1:T(8,128)(4,1)} %and_and_fusion) | copy-start | bytes 2359300
  216.6 24.6 %all-to-all-start.5 = ((bf16[32,3,8,512]{3,2,1,0:T(8,128)(2,1)}), bf16[32,3,8,512]{3,2,1,0:T(8,128)(2,1)S(1)}, u32[]{:S(2)}, u32[]{:S(2)}) async-start(bf16[32,3,8,512]{3,2,1,0:T(8,128)(2,1)} %broadcast_in_dim.18), calls=%async_computation.5 | async-start | bytes 1572864 | tf_op jit(solution)/shard_map/all_to_all | solution.py:61
  251.1 3.2 %copy-start.7 = (f32[512]{0:T(512)S(1)}, f32[512]{0:T(512)}, u32[]{:S(2)}) copy-start(f32[512]{0:T(512)} %param.15) | copy-start | bytes 6148
where the time goes:
time: 258 us; the launch traced here: 257 us
  waiting for transfers between devices  110 us (43%)
  blocking collectives  41.7 us (16%)
  starting transfers between devices  40.5 us (16%)
  matrix products  31.3 us (12%)
  local copies, waits for them, and re-layouts  17.5 us (7%)
  other arithmetic  15.2 us (6%)
    ppermute x2, waiting for transfers between devices, passed_along(): lax.ppermute(value, axis, [(source, source + steps) for source in range(f...  55.9 us
    psum x3, blocking collectives, over_axes(): value = lax.psum(value, axis)  26.2 us
    all_to_all x1, waiting for transfers between devices, shards(): lax.all_to_all(keys, 'head', split_axis=1, concat_axis=0, tiled=True)  16.1 us
    all_to_all x1, waiting for transfers between devices, copy_for_each(): lax.all_to_all(jnp.broadcast_to(value[None], (peers, *value.shape)), axis...  13.6 us
    all_to_all x1, waiting for transfers between devices, shards(): lax.all_to_all(values, 'head', split_axis=1, concat_axis=0, tiled=True)  13.2 us
    all_to_all x1, waiting for transfers between devices, shards(): lax.all_to_all(queries, 'head', split_axis=1, concat_axis=0, tiled=True)  11.4 us
    sub x1, matrix products, shards(): expo = jnp.exp(scores - peak)  10.9 us
    all_to_all x1, starting transfers between devices, shards(): lax.all_to_all(keys, 'head', split_axis=1, concat_axis=0, tiled=True)  10.9 us
  transfers between devices with their start and end apart: 7, of which 6 were waited for; matrix products, arithmetic and copies ran while one was open for 16% of the time, Pallas kernels for 0%

commit v1 on v0

v1 whole, which is shorter than its diff:
```python
import functools
import math

import jax
import jax.numpy as jnp
from jax import lax
from jax.experimental import pallas as pl
from jax.experimental.pallas import tpu as pltpu
from jax.sharding import PartitionSpec as P

AHD = 128
TQ = 128
X = 4
EPS = 1e-06
RMS_EPS = 1e-05
NEG = -1e30
MESH = pl.DeviceIdType.MESH
NT = (((1,), (1,)), ((), ()))
TN = (((0,), (0,)), ((), ()))
NN = (((1,), (0,)), ((), ()))
F32 = jnp.float32
BF16 = jnp.bfloat16


def dot(a, b, dims):
    return lax.dot_general(a, b, dims, preferred_element_type=F32)


def sigmoid(a):
    return 1.0 / (1.0 + jnp.exp(-a))


def kernel(
    sizes,
    q_in, k_in, v_in, rates, gate_in, up_in, down_in, gain,
    out,
    qbuf, kbuf, vbuf, weights, casts, hidden, target, ggate, gup,
    part, core_in, xs, x_one, x_two, y_own, y_in, gathered, renormed, attended,
    z_send, z_recv, own_sem, w_sem, h1_send, h1_recv, h2_send, h2_recv,
    c_send, c_recv, x_send, x_recv, y_send, y_recv, g_send, g_recv, gx_send, gx_recv, gc_send, gc_recv,
):
    Y, Z, T, F, B = sizes
    C = 2 * X * Y
    H = F // 2
    G = X * Y
    HY = Y // 2
    rem = lax.rem
    c = lax.axis_index("ctx")
    z = lax.axis_index("head")
    core = rem(c, 2)
    chip = lax.div(c, 2)
    y = rem(chip, Y)
    x = lax.div(chip, Y)
    other = 1 - core
    mate = (c + 1 - 2 * core, z)
    xp, xm, xo = rem(x + 1, X), rem(x + X - 1, X), rem(x + 2, X)

    def at(xx, yy):
        return ((xx * Y + yy) * 2 + core, z)

    def remote(src, dst, send, recv, device):
        return pltpu.make_async_remote_copy(
            src_ref=src, dst_ref=dst, send_sem=send, recv_sem=recv, device_id=device, device_id_type=MESH
        )

    for m, ref in enumerate((gate_in, up_in, down_in)):
        pltpu.make_async_copy(ref, weights.at[m], w_sem.at[m]).start()
    own = pl.ds(2 * T + z * B, B)
    mine = pl.ds(pl.multiple_of(z * F, F), F)
    own_copies = [
        pltpu.make_async_copy(k_in.at[:, mine], kbuf.at[own, :], own_sem.at[0]),
        pltpu.make_async_copy(v_in.at[:, mine], vbuf.at[own, :], own_sem.at[1]),
        pltpu.make_async_copy(q_in.at[:, mine], qbuf.at[pl.ds(z * B, B), :], own_sem.at[2]),
    ]
    for copy in own_copies:
        copy.start()

    barrier = pltpu.get_barrier_semaphore()
    partners = [(c, rem(z + d, Z)) for d in range(1, Z)]
    partners += [at(xp, y), at(xm, y), mate]
    partners += [at(x, rem(y + d, Y)) for d in range(1, Y)]
    partners += [(rem(c + 2, C), z), (rem(c + C - 2, C), z)]
    for partner in partners:
        pl.semaphore_signal(barrier, inc=1, device_id=partner, device_id_type=MESH)
    pl.semaphore_wait(barrier, len(partners))

    def z_copy(which, d):
        src = (k_in, v_in, q_in)[which]
        dst, base = ((kbuf, 2 * T), (vbuf, 2 * T), (qbuf, 0))[which]
        t = rem(z + d, Z)
        return remote(
            src.at[:, pl.ds(pl.multiple_of(t * F, F), F)],
            dst.at[pl.ds(base + z * B, B), :],
            z_send.at[which, d],
            z_recv.at[which, d],
            (c, t),
        )

    order = []
    for d in range(1, Z // 2):
        order += [d, Z - d]
    order.append(Z // 2)
    for d in order:
        z_copy(0, d).start()
        z_copy(1, d).start()

    @pl.when(c == 0)
    def _():
        zeros = jnp.zeros((T, F), BF16)
        kbuf[pl.ds(T, T), :] = zeros
        vbuf[pl.ds(T, T), :] = zeros

    @pl.when(c < 2)
    def _():
        zeros = jnp.zeros((T, F), BF16)
        kbuf[pl.ds(0, T), :] = zeros
        vbuf[pl.ds(0, T), :] = zeros

    for m, ref in enumerate((gate_in, up_in, down_in)):
        pltpu.make_async_copy(ref, weights.at[m], w_sem.at[m]).wait()
    for m in range(3):
        casts[m] = weights[m].astype(BF16)

    def ahead(which, s, first):
        buf = (kbuf, vbuf)[which]
        return remote(
            buf.at[pl.ds(2 * T + s * B, B), :],
            buf.at[pl.ds(s * B, B), :],
            h2_send.at[which, s],
            h2_recv.at[which, s],
            (rem(c + 2, C), z),
        )

    def across(which, s):
        buf = (kbuf, vbuf)[which]
        return remote(
            buf.at[pl.ds((1 - core) * 2 * T + s * B, B), :],
            buf.at[pl.ds(T + s * B, B), :],
            h1_send.at[which, s],
            h1_recv.at[which, s],
            mate,
        )

    def turn(i):
        return jnp.where(rem(i, 2) == 1, lax.div(i + 1, 2), rem(Z - lax.div(i, 2), Z))

    def update(i, carry):
        d = turn(i)
        s = rem(z + Z - d, Z)

        @pl.when(i == 0)
        def _():
            own_copies[0].wait()
            own_copies[1].wait()

        @pl.when(i > 0)
        def _():
            z_copy(0, d).wait_recv()
            z_copy(1, d).wait_recv()

        @pl.when(c + 2 < C)
        def _():
            ahead(0, s, 0).start()
            ahead(1, s, 0).start()

        @pl.when(core == 0)
        def _():
            across(0, s).start()
            across(1, s).start()

        rows = pl.ds(pl.multiple_of(s * B, B), B)
        here = pl.ds(pl.multiple_of(2 * T + s * B, B), B)
        k = kbuf[here, :]
        aim = (rates[rows, :] * vbuf[here, :].astype(F32)).astype(BF16)
        target[rows, :] = aim
        pre_gate = dot(k, casts[0], NN)
        pre_up = dot(k, casts[1], NN)
        back = dot(aim, casts[2], NT)
        sig = sigmoid(pre_gate)
        sil = pre_gate * sig
        hidden[rows, :] = (sil * pre_up).astype(BF16)
        ggate[rows, :] = (back * pre_up * (sig * (1.0 + pre_gate * (1.0 - sig)))).astype(BF16)
        gup[rows, :] = (back * sil).astype(BF16)
        return carry

    lax.fori_loop(0, Z, update, 0)

    for d in order:
        z_copy(2, d).start()

    here = pl.ds(2 * T, T)

    def packed(step):
        low = step[:, :H].reshape(G, 8, H)
        high = step[:, H:].reshape(G, 8, H)
        return jnp.concatenate([low, high], axis=1).astype(BF16)

    def steps(half, carry):
        cols = pl.ds(pl.multiple_of(half * H, H), H)
        rows = pl.ds(half * G, G)
        part[rows, 0:16, :] = packed(dot(ggate[:, cols], kbuf[here, :], TN))
        part[rows, 16:32, :] = packed(dot(gup[:, cols], kbuf[here, :], TN))
        part[rows, 32:48, :] = packed(dot(target[:, cols], hidden[...], TN))
        return carry

    def core_copy(j, xx):
        return remote(
            part.at[pl.ds(other * G + xx * Y, Y)],
            core_in.at[pl.ds(xx * Y, Y)],
            c_send.at[j],
            c_recv.at[j],
            mate,
        )

    blocks = (xo, xp, xm, x)
    steps(other, 0)
    for j in range(4):
        core_copy(j, blocks[j]).start()
    steps(core, 0)

    def chip_sum(j):
        xx = blocks[j]
        core_copy(j, xx).wait_recv()
        total = part[pl.ds(core * G + xx * Y, Y)].astype(F32) + core_in[pl.ds(xx * Y, Y)].astype(F32)
        return total

    def x_copy(j, xx, lo, dst, to):
        return remote(xs.at[pl.ds(xx * Y + lo, HY)], dst, x_send.at[j], x_recv.at[j], to)

    to_p, to_m = at(xp, y), at(xm, y)
    x_copies = [
        x_copy(0, xo, 0, x_one.at[0], to_p),
        x_copy(1, xo, HY, x_one.at[1], to_m),
        x_copy(2, xp, HY, x_two.at[0, pl.ds(HY, HY)], to_p),
        x_copy(3, xm, 0, x_two.at[1, pl.ds(0, HY)], to_m),
        x_copy(4, xp, 0, x_two.at[0, pl.ds(0, HY)], to_p),
        x_copy(5, xm, HY, x_two.at[1, pl.ds(HY, HY)], to_m),
    ]
    xs[pl.ds(xo * Y, Y)] = chip_sum(0).astype(BF16)
    x_copies[0].start()
    x_copies[1].start()
    sum_p = chip_sum(1)
    xs[pl.ds(xp * Y + HY, HY)] = sum_p[HY:].astype(BF16)
    x_copies[2].start()
    sum_m = chip_sum(2)
    xs[pl.ds(xm * Y, HY)] = sum_m[:HY].astype(BF16)
    x_copies[3].start()
    x_copies[0].wait_recv()
    xs[pl.ds(xp * Y, HY)] = (sum_p[:HY] + x_one[0].astype(F32)).astype(BF16)
    x_copies[4].start()
    x_copies[1].wait_recv()
    xs[pl.ds(xm * Y + HY, HY)] = (sum_m[HY:] + x_one[1].astype(F32)).astype(BF16)
    x_copies[5].start()
    y_own[...] = chip_sum(3)

    def relay(i, carry):
        s = rem(z + Z - turn(i), Z)

        @pl.when((core == 1) & (c >= 2))
        def _():
            ahead(0, s, 0).wait_recv()
            across(0, s).start()
            ahead(1, s, 0).wait_recv()
            across(1, s).start()

        return carry

    lax.fori_loop(0, Z, relay, 0)

    for j in range(2, 6):
        x_copies[j].wait_recv()
    y_own[...] = y_own[...] + x_two[0].astype(F32) + x_two[1].astype(F32)
    xs[pl.ds(x * Y, Y)] = y_own[...].astype(BF16)

    def y_copy(d):
        t = rem(y + d, Y)
        return remote(xs.at[x * Y + t], y_in.at[d - 1], y_send.at[d - 1], y_recv.at[d - 1], at(x, t))

    y_order = []
    for d in range(1, Y // 2):
        y_order += [d, Y - d]
    y_order.append(Y // 2)
    for d in y_order:
        y_copy(d).start()

    for d in order:
        z_copy(2, d).wait_recv()
    own_copies[2].wait()

    def arrived(i, carry):
        @pl.when((core == 1) | (c >= 2))
        def _():
            across(0, i).wait_recv()
            across(1, i).wait_recv()

        @pl.when((core == 0) & (c >= 2))
        def _():
            ahead(0, i, 0).wait_recv()
            ahead(1, i, 0).wait_recv()

        return carry

    lax.fori_loop(0, Z, arrived, 0)

    tiles = T // TQ
    units = (F // AHD) * tiles
    span = 2 * T + TQ
    r_at = lax.broadcasted_iota(jnp.int32, (TQ, TQ), 0)
    c_at = lax.broadcasted_iota(jnp.int32, (TQ, TQ), 1)
    after = c_at > r_at
    k_at = lax.broadcasted_iota(jnp.int32, (1, span), 1)
    factor = math.log2(math.e) / math.sqrt(AHD)

    def attend(u, carry):
        head = lax.div(u, tiles)
        start = pl.multiple_of(rem(u, tiles) * TQ, TQ)
        lanes = pl.ds(pl.multiple_of(head * AHD, AHD), AHD)
        keys = pl.ds(start, span)
        rows = pl.ds(start, TQ)
        scores = dot(qbuf[rows, lanes], kbuf[keys, lanes], NT)
        bias = jnp.where(k_at + start >= 2 * T - c * T, 0.0, NEG)
        scores = scores + bias
        first = jnp.where(after, scores[:, :TQ], NEG)
        last = jnp.where(after, NEG, scores[:, 2 * T :])
        scores = jnp.concatenate([first, scores[:, TQ : 2 * T], last], axis=1)
        peak = jnp.max(scores, axis=1, keepdims=True)
        expo = jnp.exp2((scores - peak) * factor)
        total = jnp.sum(expo, axis=1, keepdims=True)
        mixed = dot(expo.astype(BF16), vbuf[keys, lanes], NN)
        attended[rows, lanes] = mixed / total
        return carry

    cut_a, cut_b = units * 5 // 16, units * 10 // 16
    lax.fori_loop(0, cut_a, attend, 0)

    for d in y_order:
        y_copy(d).wait_recv()
    total = y_own[y]
    for d in range(1, Y):
        total = total + y_in[d - 1].astype(F32)
    owner = core * G + x * Y + y
    group = pl.ds(pl.multiple_of(lax.div(owner * 8, 128) * 128, 128), 128)
    inside = pl.multiple_of(rem(owner * 8, 128), 8)
    for m in range(3):
        weights[m, 0:128, :] = weights[m, :, group].T
        before = weights[m, pl.ds(inside, 8), :]
        norm_before = jnp.sqrt(jnp.sum(before * before, axis=1, keepdims=True) + EPS)
        low = before[:, :H] + total[m * 16 : m * 16 + 8]
        high = before[:, H:] + total[m * 16 + 8 : m * 16 + 16]
        squares = jnp.sum(low * low, axis=1, keepdims=True) + jnp.sum(high * high, axis=1, keepdims=True)
        ratio = norm_before / jnp.sqrt(squares + EPS)
        gathered[owner, m * 16 : m * 16 + 16, :] = jnp.concatenate([low * ratio, high * ratio], axis=0).astype(BF16)

    def gy_copy(d):
        return remote(gathered.at[owner], gathered.at[owner], g_send.at[d - 1], g_recv.at[d - 1], at(x, rem(y + d, Y)))

    for d in y_order:
        gy_copy(d).start()
    lax.fori_loop(cut_a, cut_b, attend, 0)
    for d in y_order:
        gy_copy(d).wait_recv()

    def gx_copy(j, xx, lo, n, to):
        group = gathered.at[pl.ds(core * G + xx * Y + lo, n)]
        return remote(group, group, gx_send.at[j], gx_recv.at[j], to)

    def gc_copy(j, xx):
        group = gathered.at[pl.ds(core * G + xx * Y, Y)]
        return remote(group, group, gc_send.at[j], gc_recv.at[j], mate)

    gx = [
        gx_copy(0, x, 0, HY, to_p),
        gx_copy(1, x, HY, HY, to_m),
        gx_copy(2, x, HY, HY, to_p),
        gx_copy(3, x, 0, HY, to_m),
        gx_copy(4, xm, 0, HY, to_p),
        gx_copy(5, xp, HY, HY, to_m),
    ]
    gc = [gc_copy(0, x), gc_copy(1, xm), gc_copy(2, xp), gc_copy(3, xo)]
    for j in range(4):
        gx[j].start()
    gc[0].start()
    gx[0].wait_recv()
    gx[4].start()
    gx[1].wait_recv()
    gx[5].start()
    lax.fori_loop(cut_b, units, attend, 0)
    gx[2].wait_recv()
    gc[1].start()
    gx[3].wait_recv()
    gc[2].start()
    gx[4].wait_recv()
    gx[5].wait_recv()
    gc[3].start()
    for j in range(4):
        gc[j].wait_recv()

    for m in range(3):
        block = gathered[:, m * 16 : m * 16 + 16, :].astype(F32)
        renormed[m, :, :H] = block[:, :8].reshape(F, H).astype(BF16)
        renormed[m, :, H:] = block[:, 8:].reshape(F, H).astype(BF16)

    def read_rows(i, carry):
        rows = pl.ds(pl.multiple_of(i * TQ, TQ), TQ)
        q = qbuf[rows, :]
        gate = dot(q, renormed[0], NT)
        up = dot(q, renormed[1], NT)
        inner = (gate * sigmoid(gate) * up).astype(BF16)
        read = dot(inner, renormed[2], NT)
        scale = lax.rsqrt(jnp.mean(read * read, axis=1, keepdims=True) + RMS_EPS)
        out[rows, :] = (attended[rows, :] + read * scale * gain[...]).astype(BF16)
        return carry

    lax.fori_loop(0, T // TQ, read_rows, 0)

    for d in order:
        for which in range(3):
            z_copy(which, d).wait_send()

    def sent(i, carry):
        @pl.when(c + 2 < C)
        def _():
            ahead(0, i, 0).wait_send()
            ahead(1, i, 0).wait_send()

        @pl.when((core == 0) | (c >= 2))
        def _():
            across(0, i).wait_send()
            across(1, i).wait_send()

        return carry

    lax.fori_loop(0, Z, sent, 0)
    for j in range(4):
        core_copy(j, blocks[j]).wait_send()
    for copy in x_copies + gx + gc:
        copy.wait_send()
    for d in y_order:
        y_copy(d).wait_send()
        gy_copy(d).wait_send()


def solution(mesh):
    C, Z = mesh.shape["ctx"], mesh.shape["head"]
    Y = C // (2 * X)

    def step(queries, keys, values, rates, fast_gate, fast_up, fast_down, out_gain):
        B = queries.shape[0]
        T, F = rates.shape[0], fast_gate.shape[-1]
        H, G = F // 2, X * Y
        dma = pltpu.SemaphoreType.DMA
        vmem = pltpu.VMEM
        any_space = pl.BlockSpec(memory_space=pl.ANY)
        in_vmem = pl.BlockSpec(memory_space=pltpu.VMEM)
        return pl.pallas_call(
            functools.partial(kernel, (Y, Z, T, F, B)),
            out_shape=jax.ShapeDtypeStruct((T, F), BF16),
            in_specs=[any_space] * 3 + [in_vmem] + [any_space] * 3 + [in_vmem],
            out_specs=in_vmem,
            scratch_shapes=[
                vmem((T, F), BF16),
                vmem((3 * T, F), BF16),
                vmem((3 * T, F), BF16),
                vmem((3, F, F), F32),
                vmem((3, F, F), BF16),
                vmem((T, F), BF16),
                vmem((T, F), BF16),
                vmem((T, F), BF16),
                vmem((T, F), BF16),
                vmem((2 * G, 48, H), BF16),
                vmem((G, 48, H), BF16),
                vmem((G, 48, H), BF16),
                vmem((2, Y // 2, 48, H), BF16),
                vmem((2, Y, 48, H), BF16),
                vmem((Y, 48, H), F32),
                vmem((Y - 1, 48, H), BF16),
                vmem((2 * G, 48, H), BF16),
                vmem((3, F, F), BF16),
                vmem((T, F), F32),
                dma((3, Z)),
                dma((3, Z)),
                dma((3,)),
                dma((3,)),
                dma((2, Z)),
                dma((2, Z)),
                dma((2, Z)),
                dma((2, Z)),
                dma((4,)),
                dma((4,)),
                dma((6,)),
                dma((6,)),
                dma((Y - 1,)),
                dma((Y - 1,)),
                dma((Y - 1,)),
                dma((Y - 1,)),
                dma((6,)),
                dma((6,)),
                dma((4,)),
                dma((4,)),
            ],
            compiler_params=pltpu.CompilerParams(
                collective_id=0, has_side_effects=True, vmem_limit_bytes=50 * 1024 * 1024
            ),
        )(
            queries, keys, values, rates,
            fast_gate.reshape(F, F), fast_up.reshape(F, F), fast_down.reshape(F, F), out_gain.reshape(1, F),
        )

    return jax.shard_map(
        step,
        mesh=mesh,
        in_specs=(
            P(("ctx", "head"), None),
            P(("ctx", "head"), None),
            P(("ctx", "head"), None),
            P("ctx", "head"),
            P("head", None, None),
            P("head", None, None),
            P("head", None, None),
            P("head"),
        ),
        out_specs=P("ctx", "head"),
        check_vma=False,
    )
```

time: 258 us -> 90 us (0.35)
  waiting for transfers between devices: 110 us -> 0 us
  Pallas kernels: 0 us -> 83.1 us
  blocking collectives: 41.7 us -> 0 us
  starting transfers between devices: 40.5 us -> 0 us
  matrix products: 31.3 us -> 0 us
  other arithmetic: 15.2 us -> 0 us
  local copies, waits for them, and re-layouts: 17.5 us -> 6.5 us
    pallas_call x0 -> x1, Pallas kernels: none -> 83.1 us  [step(): pl.pallas_call(functools.partial(kernel, (Y, Z, T, F, B)), out_shape=jax....]
    ppermute x2 -> x0, waiting for transfers between devices: 55.9 us -> none  [passed_along(): lax.ppermute(value, axis, [(source, source + steps) for source in range(f...]
    all_to_all x5 -> x0, waiting for transfers between devices: 54.3 us -> none  [the longest x1 16.1 us: shards(): lax.all_to_all(keys, 'head', split_axis=1, concat_axis=0, tiled=True)]
    all_to_all x5 -> x0, starting transfers between devices: 32.4 us -> none  [the longest x1 10.9 us: shards(): lax.all_to_all(keys, 'head', split_axis=1, concat_axis=0, tiled=True)]
    psum x3 -> x0, blocking collectives: 26.2 us -> none  [over_axes(): value = lax.psum(value, axis)]
    dot_general x9 -> x0, matrix products: 20.4 us -> none  [the longest x1 6.06 us: shards(): jnp.einsum('hqk,khd->qhd', weights, value_heads, preferred_element_type=j...]
    all_to_all x2 -> x0, blocking collectives: 15.5 us -> none  [the longest x1 8.21 us: copy_for_each(): lax.all_to_all(jnp.broadcast_to(value[None], (peers, *value.shape)), axis...]
    sub x1 -> x0, matrix products: 10.9 us -> none  [shards(): expo = jnp.exp(scores - peak)]
  transfers between devices with their start and end apart: 7 -> 0, of which waited for: 6 -> 0; matrix products, arithmetic and copies ran while one was open for 16% -> 0% of each run, Pallas kernels for 0% -> 0%
where the time goes in v1:
time: 90 us; the launch traced here: 89.6 us
  Pallas kernels  83.1 us (92%)
  local copies, waits for them, and re-layouts  6.5 us (7%)
    pallas_call x1, Pallas kernels, step(): pl.pallas_call(functools.partial(kernel, (Y, Z, T, F, B)), out_shape=jax....  83.1 us
    unnamed x14, local copies, waits for them, and re-layouts  6.5 us

profile of v1, /device:TPU:1, one launch (start us, length us, event | category | flops | bytes accessed | tf_op | source)
XLA Modules:
  0.0 89.6 jit_solution(17331365800607446724)
XLA Ops:
  0.0 0.0 copy-start.5
  0.0 0.7 copy-done.5
  0.7 0.0 copy-start.4
  0.7 0.1 copy.9.rates
  0.8 0.5 copy-done.4
  1.4 0.0 copy-start
  1.4 1.2 %copy-done = f32[1,512,512]{2,1,0:T(8,128)S(1)} copy-done((f32[1,512,512]{2,1,0:T(8,128)S(1)}, f32[1,512,512]{2,1,0:T(8,128)}, u32[]{:S(2)}) %copy-start) | copy-done | bytes 1048600
  2.6 0.0 copy-start.1
  2.6 1.0 %copy-done.1 = bf16[64,4096]{1,0:T(8,128)(2,1)S(1)} copy-done((bf16[64,4096]{1,0:T(8,128)(2,1)S(1)}, bf16[64,4096]{1,0:T(8,128)(2,1)}, u32[]{:S(2)}) %copy-start.1) | copy-done | bytes 524312
  3.6 0.0 copy-start.2
  3.6 1.0 %copy-done.2 = bf16[64,4096]{1,0:T(8,128)(2,1)S(1)} copy-done((bf16[64,4096]{1,0:T(8,128)(2,1)S(1)}, bf16[64,4096]{1,0:T(8,128)(2,1)}, u32[]{:S(2)}) %copy-start.2) | copy-done | bytes 524312
  4.7 0.0 copy-start.3
  4.7 1.0 %copy-done.3 = bf16[64,4096]{1,0:T(8,128)(2,1)S(1)} copy-done((bf16[64,4096]{1,0:T(8,128)(2,1)S(1)}, bf16[64,4096]{1,0:T(8,128)(2,1)}, u32[]{:S(2)}) %copy-start.3) | copy-done | bytes 524312
  5.7 83.1 %shard_map.82 = bf16[512,512]{1,0:T(8,128)(2,1)S(1)} custom-call(bf16[64,4096]{1,0:T(8,128)(2,1)S(1)} %copy-done.1, bf16[64,4096]{1,0:T(8,128)(2,1)S(1)} %copy-done.2, bf16[64,4096]{1,0:T(8,128)(2,1)S(1)} %copy-done.3, f32[512,1]{1,0:T(8,128)S(1)} %copy.9.rates, f32[512,512]{1,0:T(8,128)S(1)} %bitcast.4, f32[512,512]{1,0:T(8,128)} %bitcast.6, ...), custom_call_target="tpu_custom_call" | custom-call | tf_op jit(solution)/shard_map/pallas_call | solution.py:455
  88.8 0.8 copy.11
Async XLA Ops:
  0.0 0.7 copy-start.5
  0.7 0.7 copy-start.4
  1.4 1.2 %copy-start = (f32[1,512,512]{2,1,0:T(8,128)S(1)}, f32[1,512,512]{2,1,0:T(8,128)}, u32[]{:S(2)}) copy-start(f32[1,512,512]{2,1,0:T(8,128)} %param.12) | copy-start | bytes 3145732
  2.6 1.0 %copy-start.1 = (bf16[64,4096]{1,0:T(8,128)(2,1)S(1)}, bf16[64,4096]{1,0:T(8,128)(2,1)}, u32[]{:S(2)}) copy-start(bf16[64,4096]{1,0:T(8,128)(2,1)} %q_in.1) | copy-start | bytes 1572868
  3.6 1.0 %copy-start.2 = (bf16[64,4096]{1,0:T(8,128)(2,1)S(1)}, bf16[64,4096]{1,0:T(8,128)(2,1)}, u32[]{:S(2)}) copy-start(bf16[64,4096]{1,0:T(8,128)(2,1)} %k_in.1) | copy-start | bytes 1572868
  4.7 1.0 %copy-start.3 = (bf16[64,4096]{1,0:T(8,128)(2,1)S(1)}, bf16[64,4096]{1,0:T(8,128)(2,1)}, u32[]{:S(2)}) copy-start(bf16[64,4096]{1,0:T(8,128)(2,1)} %v_in.1) | copy-start | bytes 1572868

commit v2 on v1

v2 whole, which is shorter than its diff:
```python
import functools
import math

import jax
import jax.numpy as jnp
from jax import lax
from jax.experimental import pallas as pl
from jax.experimental.pallas import tpu as pltpu
from jax.sharding import PartitionSpec as P

AHD = 128
TQ = 128
X = 4
EPS = 1e-06
RMS_EPS = 1e-05
NEG = -1e30
MESH = pl.DeviceIdType.MESH
NT = (((1,), (1,)), ((), ()))
TN = (((0,), (0,)), ((), ()))
NN = (((1,), (0,)), ((), ()))
F32 = jnp.float32
BF16 = jnp.bfloat16


def dot(a, b, dims):
    return lax.dot_general(a, b, dims, preferred_element_type=F32)


def sigmoid(a):
    return 1.0 / (1.0 + jnp.exp(-a))


def kernel(
    sizes,
    q_in, k_in, v_in, rates_in, gate_in, up_in, down_in, gain,
    out,
    stage, qbuf, kv, rates, weights, casts, hidden, target, ggate, gup,
    part, core_in, xs, x_in, y_own, y_in, far_in, hop_out, hop_in, gathered, renormed, attended,
    kv_send, kv_recv, q_send, q_recv, own_sem, in_sem, w_sem, h1_send, h1_recv, h2_send, h2_recv,
    c_send, c_recv, x_send, x_recv, y_send, y_recv, g_send, g_recv, gx_send, gx_recv, gc_send, gc_recv,
):
    Y, Z, T, F, B = sizes
    C = 2 * X * Y
    H = F // 2
    G = X * Y
    rem = lax.rem
    c = lax.axis_index("ctx")
    z = lax.axis_index("head")
    core = rem(c, 2)
    chip = lax.div(c, 2)
    y = rem(chip, Y)
    x = lax.div(chip, Y)
    other = 1 - core
    mate = (c + 1 - 2 * core, z)
    xp, xm, xo = rem(x + 1, X), rem(x + X - 1, X), rem(x + 2, X)

    def at(xx, yy):
        return ((xx * Y + yy) * 2 + core, z)

    def remote(src, dst, send, recv, device):
        return pltpu.make_async_remote_copy(
            src_ref=src, dst_ref=dst, send_sem=send, recv_sem=recv, device_id=device, device_id_type=MESH
        )

    barrier = pltpu.get_barrier_semaphore()
    partners = [(c, rem(z + d, Z)) for d in range(1, Z)]
    partners += [at(xp, y), at(xm, y), at(xo, y), mate]
    partners += [at(x, rem(y + d, Y)) for d in range(1, Y)]
    partners += [(rem(c + 2, C), z), (rem(c + C - 2, C), z)]
    for partner in partners:
        pl.semaphore_signal(barrier, inc=1, device_id=partner, device_id_type=MESH)
    staging = [pltpu.make_async_copy(ref, stage.at[n], in_sem.at[n]) for n, ref in enumerate((k_in, v_in, q_in))]
    loading = [
        pltpu.make_async_copy(ref, weights.at[m], w_sem.at[m]) for m, ref in enumerate((gate_in, up_in, down_in))
    ]
    for copy in staging + loading:
        copy.start()

    pl.semaphore_wait(barrier, len(partners))

    def columns(t):
        return pl.ds(pl.multiple_of(t * F, F), F)

    def kv_copy(d):
        t = rem(z + d, Z)
        rows = pl.ds(2 * T + z * B, B)
        return remote(
            stage.at[pl.ds(0, 2), :, columns(t)], kv.at[:, rows, :], kv_send, kv_recv.at[d], (c, t)
        )

    def q_copy(d):
        t = rem(z + d, Z)
        return remote(
            stage.at[2, :, columns(t)], qbuf.at[pl.ds(z * B, B), :], q_send, q_recv, (c, t)
        )

    order = []
    for d in range(1, Z // 2):
        order += [d, Z - d]
    order.append(Z // 2)
    staging[0].wait()
    staging[1].wait()
    for d in order:
        kv_copy(d).start()
    own_kv = pltpu.make_async_copy(
        stage.at[pl.ds(0, 2), :, columns(z)], kv.at[:, pl.ds(2 * T + z * B, B), :], own_sem.at[0]
    )
    own_kv.start()

    @pl.when(c == 0)
    def _():
        zeros = jnp.zeros((T, F), BF16)
        kv[0, pl.ds(T, T), :] = zeros
        kv[1, pl.ds(T, T), :] = zeros

    @pl.when(c < 2)
    def _():
        zeros = jnp.zeros((T, F), BF16)
        kv[0, pl.ds(0, T), :] = zeros
        kv[1, pl.ds(0, T), :] = zeros

    for copy in loading:
        copy.wait()
    owner = core * G + x * Y + y
    group = pl.ds(pl.multiple_of(lax.div(owner * 8, 128) * 128, 128), 128)
    inside = pl.multiple_of(rem(owner * 8, 128), 8)
    for m in range(3):
        casts[m] = weights[m].astype(BF16)
        weights[m, 0:128, :] = weights[m, :, group].T
    rates[...] = jnp.broadcast_to(rates_in[...], (128, T)).T

    def all_of(ref, send, recv):
        return remote(ref, ref, send, recv, mate)

    def ahead(s):
        return remote(
            kv.at[:, pl.ds(2 * T + s * B, B), :],
            kv.at[:, pl.ds(s * B, B), :],
            h2_send,
            h2_recv,
            (rem(c + 2, C), z),
        )

    all_ahead = all_of(kv.at[:, pl.ds(0, T), :], h2_send, h2_recv)
    across = remote(
        kv.at[:, pl.ds((1 - core) * 2 * T, T), :], kv.at[:, pl.ds(T, T), :], h1_send, h1_recv, mate
    )

    def turn(i):
        return jnp.where(rem(i, 2) == 1, lax.div(i + 1, 2), rem(Z - lax.div(i, 2), Z))

    def update(i, carry):
        d = turn(i)
        s = rem(z + Z - d, Z)

        @pl.when(i == 0)
        def _():
            own_kv.wait()

        @pl.when(i > 0)
        def _():
            kv_copy(d).wait_recv()

        @pl.when(c + 2 < C)
        def _():
            ahead(s).start()

        rows = pl.ds(pl.multiple_of(s * B, B), B)
        here = pl.ds(pl.multiple_of(2 * T + s * B, B), B)
        k = kv[0, here, :]
        rate = jnp.concatenate([rates[rows, :]] * (F // 128), axis=1)
        aim = (rate * kv[1, here, :].astype(F32)).astype(BF16)
        target[rows, :] = aim
        pre_gate = dot(k, casts[0], NN)
        pre_up = dot(k, casts[1], NN)
        back = dot(aim, casts[2], NT)
        sig = sigmoid(pre_gate)
        sil = pre_gate * sig
        hidden[rows, :] = (sil * pre_up).astype(BF16)
        ggate[rows, :] = (back * pre_up * (sig * (1.0 + pre_gate * (1.0 - sig)))).astype(BF16)
        gup[rows, :] = (back * sil).astype(BF16)
        return carry

    lax.fori_loop(0, Z, update, 0)

    staging[2].wait()
    for d in order:
        q_copy(d).start()
    own_q = pltpu.make_async_copy(stage.at[2, :, columns(z)], qbuf.at[pl.ds(z * B, B), :], own_sem.at[1])
    own_q.start()

    here = pl.ds(2 * T, T)

    def packed(step):
        low = step[:, :H].reshape(G, 8, H)
        high = step[:, H:].reshape(G, 8, H)
        return jnp.concatenate([low, high], axis=1).astype(BF16)

    def steps(half):
        cols = pl.ds(pl.multiple_of(half * H, H), H)
        rows = pl.ds(half * G, G)
        part[rows, 0:16, :] = packed(dot(ggate[:, cols], kv[0, here, :], TN))
        part[rows, 16:32, :] = packed(dot(gup[:, cols], kv[0, here, :], TN))
        part[rows, 32:48, :] = packed(dot(target[:, cols], hidden[...], TN))

    blocks = (xp, xm, xo, x)

    def core_copy(j):
        return remote(
            part.at[pl.ds(other * G + blocks[j] * Y, Y)],
            core_in.at[pl.ds(blocks[j] * Y, Y)],
            c_send.at[j],
            c_recv.at[j],
            mate,
        )

    steps(other)
    for j in range(4):
        core_copy(j).start()
    steps(core)

    def chip_sum(j):
        core_copy(j).wait_recv()
        return part[pl.ds(core * G + blocks[j] * Y, Y)].astype(F32) + core_in[pl.ds(blocks[j] * Y, Y)].astype(F32)

    def x_copy(j):
        return remote(xs.at[pl.ds(blocks[j] * Y, Y)], x_in.at[j], x_send.at[j], x_recv.at[j], at(blocks[j], y))

    def y_copy(which, d):
        t = rem(y + d, Y)
        into = (y_in, far_in)[which]
        return remote(
            xs.at[(x, xo)[which] * Y + t], into.at[d - 1], y_send.at[which], y_recv.at[which], at(x, t)
        )

    hop = remote(hop_out, hop_in, x_send.at[2], x_recv.at[2], at(xo, y))
    all_y = all_of(y_in, y_send.at[0], y_recv.at[0])
    all_far = all_of(far_in, y_send.at[1], y_recv.at[1])
    y_order = [Y // 2]
    for d in range(Y // 2 - 1, 0, -1):
        y_order += [d, Y - d]

    for j in range(2):
        xs[pl.ds(blocks[j] * Y, Y)] = chip_sum(j).astype(BF16)
        x_copy(j).start()
    y_own[...] = chip_sum(2)
    far = y_own[y]
    xs[pl.ds(xo * Y, Y)] = y_own[...].astype(BF16)
    for d in y_order:
        y_copy(1, d).start()
    y_own[...] = chip_sum(3)

    @pl.when(core == 0)
    def _():
        across.start()

    for j in range(2):
        x_copy(j).wait_recv()
    y_own[...] = y_own[...] + x_in[0].astype(F32) + x_in[1].astype(F32)
    xs[pl.ds(x * Y, Y)] = y_own[...].astype(BF16)
    for d in y_order:
        y_copy(0, d).start()
    all_far.wait_recv()
    for d in range(1, Y):
        far = far + far_in[d - 1].astype(F32)
    hop_out[...] = far.astype(BF16)
    hop.start()

    @pl.when(c >= 2)
    def _():
        all_ahead.wait_recv()

    @pl.when((core == 1) & (c >= 2))
    def _():
        across.start()

    all_y.wait_recv()
    total = y_own[y]
    for d in range(1, Y):
        total = total + y_in[d - 1].astype(F32)
    hop.wait_recv()
    total = total + hop_in[...].astype(F32)
    for m in range(3):
        before = weights[m, pl.ds(inside, 8), :]
        norm_before = jnp.sqrt(jnp.sum(before * before, axis=1, keepdims=True) + EPS)
        low = before[:, :H] + total[m * 16 : m * 16 + 8]
        high = before[:, H:] + total[m * 16 + 8 : m * 16 + 16]
        squares = jnp.sum(low * low, axis=1, keepdims=True) + jnp.sum(high * high, axis=1, keepdims=True)
        ratio = norm_before / jnp.sqrt(squares + EPS)
        gathered[owner, m * 16 : m * 16 + 16, :] = jnp.concatenate([low * ratio, high * ratio], axis=0).astype(BF16)

    def gy_copy(which, d):
        block = gathered.at[core * G + (x, xo)[which] * Y + y]
        return remote(block, block, g_send.at[which], g_recv.at[which], at(x, rem(y + d, Y)))

    def gx_copy(j):
        group = gathered.at[pl.ds(core * G + x * Y, Y)]
        return remote(group, group, gx_send.at[j], gx_recv.at[j], at(blocks[j], y))

    def gc_copy(j):
        group = gathered.at[pl.ds(core * G + blocks[j] * Y, Y)]
        return remote(group, group, gc_send.at[j], gc_recv.at[j], mate)

    opposite = remote(gathered.at[owner], gathered.at[owner], gx_send.at[2], gx_recv.at[2], at(xo, y))
    seven = gathered.at[pl.ds(0, Y - 1)]
    all_gy = [all_of(seven, g_send.at[which], g_recv.at[which]) for which in range(2)]
    opposite.start()
    for d in y_order:
        gy_copy(0, d).start()

    all_q = all_of(qbuf.at[pl.ds(0, (Z - 1) * B), :], q_send, q_recv)
    all_q.wait_recv()
    own_q.wait()

    @pl.when((core == 1) | (c >= 2))
    def _():
        across.wait_recv()

    tiles = T // TQ
    units = (F // AHD) * tiles
    span = 2 * T + TQ
    r_at = lax.broadcasted_iota(jnp.int32, (TQ, TQ), 0)
    c_at = lax.broadcasted_iota(jnp.int32, (TQ, TQ), 1)
    after = c_at > r_at
    k_at = lax.broadcasted_iota(jnp.int32, (1, span), 1)
    factor = math.log2(math.e) / math.sqrt(AHD)

    def attend(u, carry):
        head = lax.div(u, tiles)
        start = pl.multiple_of(rem(u, tiles) * TQ, TQ)
        lanes = pl.ds(pl.multiple_of(head * AHD, AHD), AHD)
        keys = pl.ds(start, span)
        rows = pl.ds(start, TQ)
        scores = dot(qbuf[rows, lanes], kv[0, keys, lanes], NT)
        bias = jnp.where(k_at + start >= 2 * T - c * T, 0.0, NEG)
        scores = scores + bias
        first = jnp.where(after, scores[:, :TQ], NEG)
        last = jnp.where(after, NEG, scores[:, 2 * T :])
        scores = jnp.concatenate([first, scores[:, TQ : 2 * T], last], axis=1)
        peak = jnp.max(scores, axis=1, keepdims=True)
        expo = jnp.exp2((scores - peak) * factor)
        total = jnp.sum(expo, axis=1, keepdims=True)
        mixed = dot(expo.astype(BF16), kv[1, keys, lanes], NN)
        attended[rows, lanes] = mixed / total
        return carry

    cuts = [units * n // 16 for n in (0, 6, 10, 16)]
    lax.fori_loop(cuts[0], cuts[1], attend, 0)
    opposite.wait_recv()
    for d in y_order:
        gy_copy(1, d).start()
    lax.fori_loop(cuts[1], cuts[2], attend, 0)
    all_gy[0].wait_recv()
    for j in range(2):
        gx_copy(j).start()
    gc_copy(3).start()
    lax.fori_loop(cuts[2], cuts[3], attend, 0)

    all_of(kv.at[:, pl.ds(0, (Z - 1) * B), :], kv_send, h1_recv).wait_send()
    all_q.wait_send()

    @pl.when(c + 2 < C)
    def _():
        all_ahead.wait_send()

    @pl.when((core == 0) | (c >= 2))
    def _():
        across.wait_send()

    for j in range(4):
        core_copy(j).wait_send()
    for j in range(2):
        x_copy(j).wait_send()
    hop.wait_send()
    all_y.wait_send()
    all_far.wait_send()
    opposite.wait_send()
    all_gy[0].wait_send()

    for j in range(2):
        gx_copy(j).wait_recv()
        gc_copy(1 - j).start()
    all_gy[1].wait_recv()
    gc_copy(2).start()

    def unpack(half):
        rows = pl.ds(pl.multiple_of(half * H, H), H)
        for m in range(3):
            block = gathered[pl.ds(half * G, G), m * 16 : m * 16 + 16, :].astype(F32)
            renormed[m, rows, :H] = block[:, :8].reshape(H, H).astype(BF16)
            renormed[m, rows, H:] = block[:, 8:].reshape(H, H).astype(BF16)

    def inner(half):
        cols = pl.ds(pl.multiple_of(half * H, H), H)
        gate = dot(qbuf[...], renormed[0, cols, :], NT)
        up = dot(qbuf[...], renormed[1, cols, :], NT)
        hidden[:, cols] = (gate * sigmoid(gate) * up).astype(BF16)

    unpack(core)
    inner(core)
    for j in range(4):
        gc_copy(j).wait_recv()
    unpack(other)
    inner(other)

    def read_rows(i, carry):
        rows = pl.ds(pl.multiple_of(i * TQ, TQ), TQ)
        read = dot(hidden[rows, :], renormed[2], NT)
        scale = lax.rsqrt(jnp.mean(read * read, axis=1, keepdims=True) + RMS_EPS)
        out[rows, :] = (attended[rows, :] + read * scale * gain[...]).astype(BF16)
        return carry

    lax.fori_loop(0, T // TQ, read_rows, 0)

    all_gy[1].wait_send()
    for j in range(2):
        gx_copy(j).wait_send()
    for j in range(4):
        gc_copy(j).wait_send()


def solution(mesh):
    C, Z = mesh.shape["ctx"], mesh.shape["head"]
    Y = C // (2 * X)

    def step(queries, keys, values, rates, fast_gate, fast_up, fast_down, out_gain):
        B = queries.shape[0]
        T, F = rates.shape[0], fast_gate.shape[-1]
        H, G = F // 2, X * Y
        dma = pltpu.SemaphoreType.DMA
        vmem = pltpu.VMEM
        any_space = pl.BlockSpec(memory_space=pltpu.HBM)
        in_vmem = pl.BlockSpec(memory_space=pltpu.VMEM)
        return pl.pallas_call(
            functools.partial(kernel, (Y, Z, T, F, B)),
            out_shape=jax.ShapeDtypeStruct((T, F), BF16),
            in_specs=[any_space] * 3 + [in_vmem] + [any_space] * 3 + [in_vmem],
            out_specs=in_vmem,
            scratch_shapes=[
                vmem((3, B, Z * F), BF16),
                vmem((T, F), BF16),
                vmem((2, 3 * T, F), BF16),
                vmem((T, 128), F32),
                vmem((3, F, F), F32),
                vmem((3, F, F), BF16),
                vmem((T, F), BF16),
                vmem((T, F), BF16),
                vmem((T, F), BF16),
                vmem((T, F), BF16),
                vmem((2 * G, 48, H), BF16),
                vmem((G, 48, H), BF16),
                vmem((G, 48, H), BF16),
                vmem((2, Y, 48, H), BF16),
                vmem((Y, 48, H), F32),
                vmem((Y - 1, 48, H), BF16),
                vmem((Y - 1, 48, H), BF16),
                vmem((48, H), BF16),
                vmem((48, H), BF16),
                vmem((2 * G, 48, H), BF16),
                vmem((3, F, F), BF16),
                vmem((T, F), F32),
                dma,
                dma((Z,)),
                dma,
                dma,
                dma((2,)),
                dma((3,)),
                dma((3,)),
                dma,
                dma,
                dma,
                dma,
                dma((4,)),
                dma((4,)),
                dma((3,)),
                dma((3,)),
                dma((2,)),
                dma((2,)),
                dma((2,)),
                dma((2,)),
                dma((3,)),
                dma((3,)),
                dma((4,)),
                dma((4,)),
            ],
            compiler_params=pltpu.CompilerParams(
                collective_id=0, has_side_effects=True, vmem_limit_bytes=56 * 1024 * 1024
            ),
        )(
            queries, keys, values, rates.reshape(1, T),
            fast_gate.reshape(F, F), fast_up.reshape(F, F), fast_down.reshape(F, F), out_gain.reshape(1, F),
        )

    return jax.shard_map(
        step,
        mesh=mesh,
        in_specs=(
            P(("ctx", "head"), None),
            P(("ctx", "head"), None),
            P(("ctx", "head"), None),
            P("ctx", "head"),
            P("head", None, None),
            P("head", None, None),
            P("head", None, None),
            P("head"),
        ),
        out_specs=P("ctx", "head"),
        check_vma=False,
    )
```

time: 90 us -> 76.8 us (0.85)
  Pallas kernels: 83.1 us -> 74.8 us
  local copies, waits for them, and re-layouts: 6.5 us -> 1.87 us
    pallas_call x1, Pallas kernels: 83.1 us -> 74.8 us  [step(): pl.pallas_call(functools.partial(kernel, (Y, Z, T, F, B)), out_shape=jax....]
    unnamed x14 -> x1, local copies, waits for them, and re-layouts: 6.5 us -> 1.87 us
where the time goes in v2:
time: 76.8 us; the launch traced here: 76.6 us
  Pallas kernels  74.8 us (97%)
  local copies, waits for them, and re-layouts  1.87 us (2%)
    pallas_call x1, Pallas kernels, step(): pl.pallas_call(functools.partial(kernel, (Y, Z, T, F, B)), out_shape=jax....  74.8 us
    unnamed x1, local copies, waits for them, and re-layouts  1.87 us

profile of v2, /device:TPU:1, one launch (start us, length us, event | category | flops | bytes accessed | tf_op | source)
XLA Modules:
  0.0 76.6 jit_solution(11565699947623183613)
XLA Ops:
  0.0 74.8 %shard_map.82 = bf16[512,512]{1,0:T(8,128)(2,1)} custom-call(bf16[64,4096]{1,0:T(8,128)(2,1)} %q_in.1, bf16[64,4096]{1,0:T(8,128)(2,1)} %k_in.1, bf16[64,4096]{1,0:T(8,128)(2,1)} %v_in.1, f32[1,512]{1,0:T(1,128)} %bitcast.8, f32[512,512]{1,0:T(8,128)} %bitcast.5, f32[512,512]{1,0:T(8,128)} %bitcast.6, f32[512,512]{1,0:T(8,128)} %bitcast.7, f32[1,512]{1,0:T(1,128)} %bitcast.9), custom_call_target="tpu_custom_call" | custom-call | tf_op jit(solution)/shard_map/pallas_call | solution.py:434
  74.8 1.9 %copy.10 = bf16[512,512]{1,0:T(8,128)(2,1)} copy(bf16[512,512]{1,0:T(8,128)(2,1)} %shard_map.82) | data formatting | bytes 1048576

commit v3 on v2

--- a/solution.py
+++ b/solution.py
@@ -37,12 +37,13 @@
     stage, qbuf, kv, rates, weights, casts, hidden, target, ggate, gup,
     part, core_in, xs, x_in, y_own, y_in, far_in, hop_out, hop_in, gathered, renormed, attended,
     kv_send, kv_recv, q_send, q_recv, own_sem, in_sem, w_sem, h1_send, h1_recv, h2_send, h2_recv,
-    c_send, c_recv, x_send, x_recv, y_send, y_recv, g_send, g_recv, gx_send, gx_recv, gc_send, gc_recv,
+    c_send, c_recv, hop_send, hop_recv, x_send, x_recv, y_send, y_recv, g_send, g_recv, gx_send, gx_recv, gc_send, gc_recv,
 ):
     Y, Z, T, F, B = sizes
     C = 2 * X * Y
     H = F // 2
     G = X * Y
+    HY = Y // 2
     rem = lax.rem
     c = lax.axis_index("ctx")
     z = lax.axis_index("head")
@@ -223,43 +224,60 @@
         core_copy(j).wait_recv()
         return part[pl.ds(core * G + blocks[j] * Y, Y)].astype(F32) + core_in[pl.ds(blocks[j] * Y, Y)].astype(F32)
 
-    def x_copy(j):
-        return remote(xs.at[pl.ds(blocks[j] * Y, Y)], x_in.at[j], x_send.at[j], x_recv.at[j], at(blocks[j], y))
-
-    def y_copy(which, d):
-        t = rem(y + d, Y)
+    def half_of(xx, side):
+        return pl.ds(xx * Y + side * HY, HY)
+
+    def x_copy(j, side):
+        return remote(
+            xs.at[half_of(blocks[j], side)],
+            x_in.at[j, pl.ds(side * HY, HY)],
+            x_send.at[j, side],
+            x_recv.at[j, side],
+            at(blocks[j], y),
+        )
+
+    def y_copy(which, t):
         into = (y_in, far_in)[which]
         return remote(
-            xs.at[(x, xo)[which] * Y + t], into.at[d - 1], y_send.at[which], y_recv.at[which], at(x, t)
-        )
-
-    hop = remote(hop_out, hop_in, x_send.at[2], x_recv.at[2], at(xo, y))
+            xs.at[(x, xo)[which] * Y + t],
+            into.at[rem(t - y + Y, Y) - 1],
+            y_send.at[which],
+            y_recv.at[which],
+            at(x, t),
+        )
+
+    hop = remote(hop_out, hop_in, hop_send.at[0], hop_recv.at[0], at(xo, y))
     all_y = all_of(y_in, y_send.at[0], y_recv.at[0])
     all_far = all_of(far_in, y_send.at[1], y_recv.at[1])
-    y_order = [Y // 2]
-    for d in range(Y // 2 - 1, 0, -1):
-        y_order += [d, Y - d]
+    near = lax.div(y, HY)
+    sides = (1 - near, near)
+    others = [(1 - near) * HY + e for e in range(HY)]
+    close = [near * HY + rem(y + e, HY) for e in range(1, HY)]
 
     for j in range(2):
         xs[pl.ds(blocks[j] * Y, Y)] = chip_sum(j).astype(BF16)
-        x_copy(j).start()
+        x_copy(j, sides[0]).start()
+    for j in range(2):
+        x_copy(j, sides[1]).start()
     y_own[...] = chip_sum(2)
     far = y_own[y]
     xs[pl.ds(xo * Y, Y)] = y_own[...].astype(BF16)
-    for d in y_order:
-        y_copy(1, d).start()
+    for t in others + close:
+        y_copy(1, t).start()
     y_own[...] = chip_sum(3)
 
     @pl.when(core == 0)
     def _():
         across.start()
 
-    for j in range(2):
-        x_copy(j).wait_recv()
-    y_own[...] = y_own[...] + x_in[0].astype(F32) + x_in[1].astype(F32)
-    xs[pl.ds(x * Y, Y)] = y_own[...].astype(BF16)
-    for d in y_order:
-        y_copy(0, d).start()
+    for side, peers in zip(sides, (others, close)):
+        rows = pl.ds(side * HY, HY)
+        for j in range(2):
+            x_copy(j, side).wait_recv()
+        y_own[rows] = y_own[rows] + x_in[0, rows].astype(F32) + x_in[1, rows].astype(F32)
+        xs[half_of(x, side)] = y_own[rows].astype(BF16)
+        for t in peers:
+            y_copy(0, t).start()
     all_far.wait_recv()
     for d in range(1, Y):
         far = far + far_in[d - 1].astype(F32)
@@ -279,6 +297,7 @@
     for d in range(1, Y):
         total = total + y_in[d - 1].astype(F32)
     hop.wait_recv()
+    hop.wait_send()
     total = total + hop_in[...].astype(F32)
     for m in range(3):
         before = weights[m, pl.ds(inside, 8), :]
@@ -289,24 +308,27 @@
         ratio = norm_before / jnp.sqrt(squares + EPS)
         gathered[owner, m * 16 : m * 16 + 16, :] = jnp.concatenate([low * ratio, high * ratio], axis=0).astype(BF16)
 
-    def gy_copy(which, d):
+    def gy_copy(which, t, sem):
         block = gathered.at[core * G + (x, xo)[which] * Y + y]
-        return remote(block, block, g_send.at[which], g_recv.at[which], at(x, rem(y + d, Y)))
-
-    def gx_copy(j):
-        group = gathered.at[pl.ds(core * G + x * Y, Y)]
-        return remote(group, group, gx_send.at[j], gx_recv.at[j], at(blocks[j], y))
+        return remote(block, block, g_send.at[sem], g_recv.at[sem], at(x, t))
+
+    def gx_copy(j, side):
+        group = gathered.at[pl.ds(core * G + x * Y + side * HY, HY)]
+        return remote(group, group, gx_send.at[j, side], gx_recv.at[j, side], at(blocks[j], y))
 
     def gc_copy(j):
         group = gathered.at[pl.ds(core * G + blocks[j] * Y, Y)]
         return remote(group, group, gc_send.at[j], gc_recv.at[j], mate)
 
-    opposite = remote(gathered.at[owner], gathered.at[owner], gx_send.at[2], gx_recv.at[2], at(xo, y))
-    seven = gathered.at[pl.ds(0, Y - 1)]
-    all_gy = [all_of(seven, g_send.at[which], g_recv.at[which]) for which in range(2)]
+    opposite = remote(gathered.at[owner], gathered.at[owner], hop_send.at[1], hop_recv.at[1], at(xo, y))
+    all_gy = [
+        all_of(gathered.at[pl.ds(0, n)], g_send.at[sem], g_recv.at[sem]) for sem, n in enumerate((HY - 1, HY, Y - 1))
+    ]
     opposite.start()
-    for d in y_order:
-        gy_copy(0, d).start()
+    for t in close:
+        gy_copy(0, t, 0).start()
+    for t in others:
+        gy_copy(0, t, 1).start()
 
     all_q = all_of(qbuf.at[pl.ds(0, (Z - 1) * B), :], q_send, q_recv)
     all_q.wait_recv()
@@ -344,17 +366,21 @@
         attended[rows, lanes] = mixed / total
         return carry
 
-    cuts = [units * n // 16 for n in (0, 6, 10, 16)]
+    cuts = [units * n // 16 for n in (0, 5, 8, 9, 16)]
     lax.fori_loop(cuts[0], cuts[1], attend, 0)
     opposite.wait_recv()
-    for d in y_order:
-        gy_copy(1, d).start()
+    for t in others + close:
+        gy_copy(1, t, 2).start()
     lax.fori_loop(cuts[1], cuts[2], attend, 0)
     all_gy[0].wait_recv()
     for j in range(2):
-        gx_copy(j).start()
+        gx_copy(j, near).start()
+    lax.fori_loop(cuts[2], cuts[3], attend, 0)
+    all_gy[1].wait_recv()
+    for j in range(2):
+        gx_copy(j, 1 - near).start()
     gc_copy(3).start()
-    lax.fori_loop(cuts[2], cuts[3], attend, 0)
+    lax.fori_loop(cuts[3], cuts[4], attend, 0)
 
     all_of(kv.at[:, pl.ds(0, (Z - 1) * B), :], kv_send, h1_recv).wait_send()
     all_q.wait_send()
@@ -370,17 +396,19 @@
     for j in range(4):
         core_copy(j).wait_send()
     for j in range(2):
-        x_copy(j).wait_send()
-    hop.wait_send()
+        for side in range(2):
+            x_copy(j, side).wait_send()
     all_y.wait_send()
     all_far.wait_send()
     opposite.wait_send()
     all_gy[0].wait_send()
-
-    for j in range(2):
-        gx_copy(j).wait_recv()
+    all_gy[1].wait_send()
+
+    for j in range(2):
+        for side in sides:
+            gx_copy(j, side).wait_recv()
         gc_copy(1 - j).start()
-    all_gy[1].wait_recv()
+    all_gy[2].wait_recv()
     gc_copy(2).start()
 
     def unpack(half):
@@ -412,9 +440,10 @@
 
     lax.fori_loop(0, T // TQ, read_rows, 0)
 
-    all_gy[1].wait_send()
-    for j in range(2):
-        gx_copy(j).wait_send()
+    all_gy[2].wait_send()
+    for j in range(2):
+        for side in range(2):
+            gx_copy(j, side).wait_send()
     for j in range(4):
         gc_copy(j).wait_send()
 
@@ -472,19 +501,21 @@
                 dma,
                 dma((4,)),
                 dma((4,)),
-                dma((3,)),
-                dma((3,)),
                 dma((2,)),
                 dma((2,)),
+                dma((2, 2)),
+                dma((2, 2)),
                 dma((2,)),
                 dma((2,)),
                 dma((3,)),
                 dma((3,)),
+                dma((2, 2)),
+                dma((2, 2)),
                 dma((4,)),
                 dma((4,)),
             ],
             compiler_params=pltpu.CompilerParams(
-                collective_id=0, has_side_effects=True, vmem_limit_bytes=56 * 1024 * 1024
+                collective_id=0, has_side_effects=True, vmem_limit_bytes=54640 * 1024
             ),
         )(
             queries, keys, values, rates.reshape(1, T),

time: 76.8 us -> 74.5 us (0.970)
  Pallas kernels: 74.8 us -> 72.5 us
    pallas_call x1, Pallas kernels: 74.8 us -> 72.5 us  [step(): pl.pallas_call(functools.partial(kernel, (Y, Z, T, F, B)), out_shape=jax....]
    unnamed x1 -> x5, local copies, waits for them, and re-layouts: 1.87 us -> 1.49 us
where the time goes in v3:
time: 74.5 us; the launch traced here: 74 us
  Pallas kernels  72.5 us (97%)
  local copies, waits for them, and re-layouts  1.49 us (2%)
    pallas_call x1, Pallas kernels, step(): pl.pallas_call(functools.partial(kernel, (Y, Z, T, F, B)), out_shape=jax....  72.5 us
    unnamed x5, local copies, waits for them, and re-layouts  1.49 us

profile of v3, /device:TPU:1, one launch (start us, length us, event | category | flops | bytes accessed | tf_op | source)
XLA Modules:
  0.0 74.0 jit_solution(5071302943501768271)
XLA Ops:
  0.0 0.0 copy-start.1
  0.0 0.0 copy-start
  0.0 0.7 copy-done.1
  0.7 0.0 copy-done
  0.7 72.5 %shard_map.82 = bf16[512,512]{1,0:T(8,128)(2,1)S(1)} custom-call(bf16[64,4096]{1,0:T(8,128)(2,1)} %q_in.1, bf16[64,4096]{1,0:T(8,128)(2,1)} %k_in.1, bf16[64,4096]{1,0:T(8,128)(2,1)} %v_in.1, f32[1,512]{1,0:T(1,128)S(1)} %bitcast.5, f32[512,512]{1,0:T(8,128)} %bitcast.7, f32[512,512]{1,0:T(8,128)} %bitcast.8, f32[512,512]{1,0:T(8,128)} %bitcast.9, ...), custom_call_target="tpu_custom_call" | custom-call | tf_op jit(solution)/shard_map/pallas_call | solution.py:463
  73.2 0.8 %copy.10 = bf16[512,512]{1,0:T(8,128)(2,1)} copy(bf16[512,512]{1,0:T(8,128)(2,1)S(1)} %shard_map.82) | data formatting | bytes 1048576
Async XLA Ops:
  0.0 0.7 copy-start.1
  0.0 0.7 copy-start

commit v4 on v3

--- a/solution.py
+++ b/solution.py
@@ -9,7 +9,7 @@
 from jax.sharding import PartitionSpec as P
 
 AHD = 128
-TQ = 128
+TQ = 256
 X = 4
 EPS = 1e-06
 RMS_EPS = 1e-05
@@ -32,9 +32,9 @@
 
 def kernel(
     sizes,
-    q_in, k_in, v_in, rates_in, gate_in, up_in, down_in, gain,
+    q_in, k_in, v_in, rates_in, gate_in, up_in, down_in, gain_in,
     out,
-    stage, qbuf, kv, rates, weights, casts, hidden, target, ggate, gup,
+    stage, qbuf, kv, rate_row, gain, rates, weights, casts, hidden, target, ggate, gup,
     part, core_in, xs, x_in, y_own, y_in, far_in, hop_out, hop_in, gathered, renormed, attended,
     kv_send, kv_recv, q_send, q_recv, own_sem, in_sem, w_sem, h1_send, h1_recv, h2_send, h2_recv,
     c_send, c_recv, hop_send, hop_recv, x_send, x_recv, y_send, y_recv, g_send, g_recv, gx_send, gx_recv, gc_send, gc_recv,
@@ -63,6 +63,11 @@
             src_ref=src, dst_ref=dst, send_sem=send, recv_sem=recv, device_id=device, device_id_type=MESH
         )
 
+    staging = [pltpu.make_async_copy(ref, stage.at[n], in_sem.at[n]) for n, ref in enumerate((k_in, v_in, q_in))]
+    sources = ((gate_in, weights.at[0]), (up_in, weights.at[1]), (down_in, weights.at[2]), (rates_in, rate_row), (gain_in, gain))
+    loading = [pltpu.make_async_copy(src, dst, w_sem.at[m]) for m, (src, dst) in enumerate(sources)]
+    staging[0].start()
+    staging[1].start()
     barrier = pltpu.get_barrier_semaphore()
     partners = [(c, rem(z + d, Z)) for d in range(1, Z)]
     partners += [at(xp, y), at(xm, y), at(xo, y), mate]
@@ -70,13 +75,8 @@
     partners += [(rem(c + 2, C), z), (rem(c + C - 2, C), z)]
     for partner in partners:
         pl.semaphore_signal(barrier, inc=1, device_id=partner, device_id_type=MESH)
-    staging = [pltpu.make_async_copy(ref, stage.at[n], in_sem.at[n]) for n, ref in enumerate((k_in, v_in, q_in))]
-    loading = [
-        pltpu.make_async_copy(ref, weights.at[m], w_sem.at[m]) for m, ref in enumerate((gate_in, up_in, down_in))
-    ]
-    for copy in staging + loading:
+    for copy in loading + staging[2:]:
         copy.start()
-
     pl.semaphore_wait(barrier, len(partners))
 
     def columns(t):
@@ -128,7 +128,7 @@
     for m in range(3):
         casts[m] = weights[m].astype(BF16)
         weights[m, 0:128, :] = weights[m, :, group].T
-    rates[...] = jnp.broadcast_to(rates_in[...], (128, T)).T
+    rates[...] = jnp.broadcast_to(rate_row[...], (128, T)).T
 
     def all_of(ref, send, recv):
         return remote(ref, ref, send, recv, mate)
@@ -366,7 +366,7 @@
         attended[rows, lanes] = mixed / total
         return carry
 
-    cuts = [units * n // 16 for n in (0, 5, 8, 9, 16)]
+    cuts = [units * n // 16 for n in (0, 6, 8, 10, 16)]
     lax.fori_loop(cuts[0], cuts[1], attend, 0)
     opposite.wait_recv()
     for t in others + close:
@@ -463,12 +463,14 @@
         return pl.pallas_call(
             functools.partial(kernel, (Y, Z, T, F, B)),
             out_shape=jax.ShapeDtypeStruct((T, F), BF16),
-            in_specs=[any_space] * 3 + [in_vmem] + [any_space] * 3 + [in_vmem],
+            in_specs=[any_space] * 8,
             out_specs=in_vmem,
             scratch_shapes=[
                 vmem((3, B, Z * F), BF16),
                 vmem((T, F), BF16),
                 vmem((2, 3 * T, F), BF16),
+                vmem((1, T), F32),
+                vmem((1, F), F32),
                 vmem((T, 128), F32),
                 vmem((3, F, F), F32),
                 vmem((3, F, F), BF16),
@@ -494,7 +496,7 @@
                 dma,
                 dma((2,)),
                 dma((3,)),
-                dma((3,)),
+                dma((5,)),
                 dma,
                 dma,
                 dma,
@@ -518,8 +520,8 @@
                 collective_id=0, has_side_effects=True, vmem_limit_bytes=54640 * 1024
             ),
         )(
-            queries, keys, values, rates.reshape(1, T),
-            fast_gate.reshape(F, F), fast_up.reshape(F, F), fast_down.reshape(F, F), out_gain.reshape(1, F),
+            queries, keys, values, pltpu.with_memory_space_constraint(rates.reshape(1, T), pltpu.HBM),
+            fast_gate.reshape(F, F), fast_up.reshape(F, F), fast_down.reshape(F, F), pltpu.with_memory_space_constraint(out_gain.reshape(1, F), pltpu.HBM),
         )
 
     return jax.shard_map(

time: 74.5 us -> 72.5 us (0.973)
  Pallas kernels: 72.5 us -> 71.6 us
    pallas_call x1, Pallas kernels: 72.5 us -> 71.6 us  [step(): pl.pallas_call(functools.partial(kernel, (Y, Z, T, F, B)), out_shape=jax....]
    unnamed x5 -> x1, local copies, waits for them, and re-layouts: 1.49 us -> 0.8 us
where the time goes in v4:
time: 72.5 us; the launch traced here: 72.4 us
  Pallas kernels  71.6 us (99%)
  local copies, waits for them, and re-layouts  0.8 us (1%)
    pallas_call x1, Pallas kernels, step(): pl.pallas_call(functools.partial(kernel, (Y, Z, T, F, B)), out_shape=jax....  71.6 us

profile of v4, /device:TPU:1, one launch (start us, length us, event | category | flops | bytes accessed | tf_op | source)
XLA Modules:
  0.0 72.4 jit_solution(16568010851110425149)
XLA Ops:
  0.0 71.6 %shard_map.82 = bf16[512,512]{1,0:T(8,128)(2,1)S(1)} custom-call(bf16[64,4096]{1,0:T(8,128)(2,1)} %q_in.1, bf16[64,4096]{1,0:T(8,128)(2,1)} %k_in.1, bf16[64,4096]{1,0:T(8,128)(2,1)} %v_in.1, f32[1,512]{1,0:T(1,128)} %bitcast.8, f32[512,512]{1,0:T(8,128)} %bitcast.5, f32[512,512]{1,0:T(8,128)} %bitcast.6, f32[512,512]{1,0:T(8,128)} %bitcast.7, f32[1,512]{1,0:T(1,128)} %bitcast.9), custom_call_target="tpu_custom_call" | custom-call | tf_op jit(solution)/shard_map/pallas_call | solution.py:463
  71.6 0.8 %copy.10 = bf16[512,512]{1,0:T(8,128)(2,1)} copy(bf16[512,512]{1,0:T(8,128)(2,1)S(1)} %shard_map.82) | data formatting | bytes 1048576

commit v5 on v4

--- a/solution.py
+++ b/solution.py
@@ -316,9 +316,9 @@
         group = gathered.at[pl.ds(core * G + x * Y + side * HY, HY)]
         return remote(group, group, gx_send.at[j, side], gx_recv.at[j, side], at(blocks[j], y))
 
-    def gc_copy(j):
-        group = gathered.at[pl.ds(core * G + blocks[j] * Y, Y)]
-        return remote(group, group, gc_send.at[j], gc_recv.at[j], mate)
+    def gc_copy(j, side):
+        group = gathered.at[pl.ds(core * G + blocks[j] * Y + side * HY, HY)]
+        return remote(group, group, gc_send.at[j, side], gc_recv.at[j, side], mate)
 
     opposite = remote(gathered.at[owner], gathered.at[owner], hop_send.at[1], hop_recv.at[1], at(xo, y))
     all_gy = [
@@ -379,7 +379,8 @@
     all_gy[1].wait_recv()
     for j in range(2):
         gx_copy(j, 1 - near).start()
-    gc_copy(3).start()
+    for side in sides:
+        gc_copy(3, side).start()
     lax.fori_loop(cuts[3], cuts[4], attend, 0)
 
     all_of(kv.at[:, pl.ds(0, (Z - 1) * B), :], kv_send, h1_recv).wait_send()
@@ -404,12 +405,13 @@
     all_gy[0].wait_send()
     all_gy[1].wait_send()
 
-    for j in range(2):
-        for side in sides:
+    for side in (near, 1 - near):
+        for j in range(2):
             gx_copy(j, side).wait_recv()
-        gc_copy(1 - j).start()
+            gc_copy(1 - j, side).start()
     all_gy[2].wait_recv()
-    gc_copy(2).start()
+    for side in sides:
+        gc_copy(2, side).start()
 
     def unpack(half):
         rows = pl.ds(pl.multiple_of(half * H, H), H)
@@ -427,7 +429,8 @@
     unpack(core)
     inner(core)
     for j in range(4):
-        gc_copy(j).wait_recv()
+        for side in sides:
+            gc_copy(j, side).wait_recv()
     unpack(other)
     inner(other)
 
@@ -445,7 +448,8 @@
         for side in range(2):
             gx_copy(j, side).wait_send()
     for j in range(4):
-        gc_copy(j).wait_send()
+        for side in sides:
+            gc_copy(j, side).wait_send()
 
 
 def solution(mesh):
@@ -513,8 +517,8 @@
                 dma((3,)),
                 dma((2, 2)),
                 dma((2, 2)),
-                dma((4,)),
-                dma((4,)),
+                dma((4, 2)),
+                dma((4, 2)),
             ],
             compiler_params=pltpu.CompilerParams(
                 collective_id=0, has_side_effects=True, vmem_limit_bytes=54640 * 1024

time: 72.5 us -> 72.3 us (level)
  no operation moved by 1% of the time
where the time goes in v5:
time: 72.3 us; the launch traced here: 72.2 us
  Pallas kernels  71.4 us (99%)
  local copies, waits for them, and re-layouts  0.8 us (1%)
    pallas_call x1, Pallas kernels, step(): pl.pallas_call(functools.partial(kernel, (Y, Z, T, F, B)), out_shape=jax....  71.4 us

profile of v5, /device:TPU:1, one launch (start us, length us, event | category | flops | bytes accessed | tf_op | source)
XLA Modules:
  0.0 72.2 jit_solution(3107528374152745281)
XLA Ops:
  0.0 71.4 %shard_map.82 = bf16[512,512]{1,0:T(8,128)(2,1)S(1)} custom-call(bf16[64,4096]{1,0:T(8,128)(2,1)} %q_in.1, bf16[64,4096]{1,0:T(8,128)(2,1)} %k_in.1, bf16[64,4096]{1,0:T(8,128)(2,1)} %v_in.1, f32[1,512]{1,0:T(1,128)} %bitcast.8, f32[512,512]{1,0:T(8,128)} %bitcast.5, f32[512,512]{1,0:T(8,128)} %bitcast.6, f32[512,512]{1,0:T(8,128)} %bitcast.7, f32[1,512]{1,0:T(1,128)} %bitcast.9), custom_call_target="tpu_custom_call" | custom-call | tf_op jit(solution)/shard_map/pallas_call | solution.py:467
  71.4 0.8 %copy.10 = bf16[512,512]{1,0:T(8,128)(2,1)} copy(bf16[512,512]{1,0:T(8,128)(2,1)S(1)} %shard_map.82) | data formatting | bytes 1048576

commit v6 on v5

--- a/solution.py
+++ b/solution.py
@@ -284,14 +284,6 @@
     hop_out[...] = far.astype(BF16)
     hop.start()
 
-    @pl.when(c >= 2)
-    def _():
-        all_ahead.wait_recv()
-
-    @pl.when((core == 1) & (c >= 2))
-    def _():
-        across.start()
-
     all_y.wait_recv()
     total = y_own[y]
     for d in range(1, Y):
@@ -329,6 +321,14 @@
         gy_copy(0, t, 0).start()
     for t in others:
         gy_copy(0, t, 1).start()
+
+    @pl.when(c >= 2)
+    def _():
+        all_ahead.wait_recv()
+
+    @pl.when((core == 1) & (c >= 2))
+    def _():
+        across.start()
 
     all_q = all_of(qbuf.at[pl.ds(0, (Z - 1) * B), :], q_send, q_recv)
     all_q.wait_recv()

time: 72.3 us -> 72.3 us (level)
  no operation moved by 1% of the time
where the time goes in v6:
time: 72.3 us; the launch traced here: 72.2 us
  Pallas kernels  71.4 us (99%)
  local copies, waits for them, and re-layouts  0.8 us (1%)
    pallas_call x1, Pallas kernels, step(): pl.pallas_call(functools.partial(kernel, (Y, Z, T, F, B)), out_shape=jax....  71.4 us

profile of v6, /device:TPU:1, one launch (start us, length us, event | category | flops | bytes accessed | tf_op | source)
XLA Modules:
  0.0 72.2 jit_solution(7632922296325489156)
XLA Ops:
  0.0 71.4 %shard_map.82 = bf16[512,512]{1,0:T(8,128)(2,1)S(1)} custom-call(bf16[64,4096]{1,0:T(8,128)(2,1)} %q_in.1, bf16[64,4096]{1,0:T(8,128)(2,1)} %k_in.1, bf16[64,4096]{1,0:T(8,128)(2,1)} %v_in.1, f32[1,512]{1,0:T(1,128)} %bitcast.8, f32[512,512]{1,0:T(8,128)} %bitcast.5, f32[512,512]{1,0:T(8,128)} %bitcast.6, f32[512,512]{1,0:T(8,128)} %bitcast.7, f32[1,512]{1,0:T(1,128)} %bitcast.9), custom_call_target="tpu_custom_call" | custom-call | tf_op jit(solution)/shard_map/pallas_call | solution.py:467
  71.4 0.8 %copy.10 = bf16[512,512]{1,0:T(8,128)(2,1)} copy(bf16[512,512]{1,0:T(8,128)(2,1)S(1)} %shard_map.82) | data formatting | bytes 1048576
